TPU v7x, 128 devices: a whole 4x4x4 slice. The times are simulated.
128 devices in a mesh: node: 16 (over x, z), local: 8 (over y, core).
Axes of the slice: x: 4, y: 4, z: 4, core: 2. Of those that a mesh axis runs over, the one named last changes fastest.
Arguments:
- owner_map: int32 [128], replicated, may hold values from 0 to 127, as said below
- bag_sizes: int32 [128, 8192], P(('node', 'local')), may hold values from 1 to 8
- indices: int32 [128, 8192, 8], P(('node', 'local')), may hold values from 0 to 2047
- tables: bfloat16 [262144, 128], P(('node', 'local')), may hold values from -2 to 2
- cross_down: bfloat16 [128, 128, 512], P('local'), may hold values from -0.046875 to 0.046875
- cross_up: bfloat16 [512, 128, 128], P(None, 'local'), may hold values from -0.25 to 0.25
- cross_bias: float32 [128, 128], P('local'), may hold values from -3 to 3
- mlp_weight: bfloat16 [128, 128, 2048], P('local'), may hold values from -0.046875 to 0.046875
- mlp_bias: float32 [2048], replicated, may hold values from -3 to 3
- hidden_grad: bfloat16 [8192, 2048], P('node'), may hold values from -6 to 6
Outputs:
- crossed: bfloat16 [128, 8192, 128], P('local', 'node')
- hidden: bfloat16 [8192, 2048], P('node', 'local')
- table_grad: float32 [262144, 128], P(('node', 'local'))
Inputs may be any that keep to these rules, and one draw needn't show every extreme that they name: owner_map is a permutation of the devices: each device owns exactly one feature. Call f // 16 the group of feature f; the devices with one local index own at most 3 features of one group, and exactly 3 for some local index and group in every draw.
All inputs are finite; a program needn't handle non-finite values.
Results may differ from a plain program's by a relative error of at most 0.015.
Values may be sent and summed in bfloat16 or wider, within the bound.
A program may use at most 128 MiB of HBM per device.

v0:
```python
import jax
import jax.numpy as jnp
from jax import lax
from jax.sharding import PartitionSpec as P


def bag_matrix(picks, counts, row_ids):
    matrix = jnp.zeros((picks.shape[0], row_ids.shape[0]), jnp.bfloat16)
    for column in range(picks.shape[1]):
        hit = (picks[:, column : column + 1] == row_ids[None, :]) & (counts[:, None] > column)
        matrix = matrix + hit.astype(jnp.bfloat16)
    return matrix


def on_device(
    owner_map,
    bag_sizes,
    indices,
    tables,
    cross_down,
    cross_up,
    cross_bias,
    mlp_weight,
    mlp_bias,
    hidden_grad,
):
    node_count = lax.axis_size("node")
    lane_count = lax.axis_size("local")
    my_lane = lax.axis_index("local")
    capacity = node_count // lane_count + 1
    slot_total = lane_count * capacity
    samples = hidden_grad.shape[0]
    batch_total = indices.shape[1]
    bag_depth = indices.shape[2]
    emb_width = tables.shape[1]
    rows_here = tables.shape[0]
    hidden_width = hidden_grad.shape[1]
    share_width = hidden_width // lane_count
    turns = batch_total // samples
    row_ids = jnp.arange(rows_here, dtype=jnp.int32)
    pick_blocks = indices[0].reshape(turns, samples, bag_depth)
    count_blocks = bag_sizes[0].reshape(turns, samples)

    def pool_block(inputs):
        picks, counts = inputs
        matrix = bag_matrix(picks, counts, row_ids)
        return jnp.dot(matrix, tables, preferred_element_type=jnp.float32).astype(jnp.bfloat16)

    pooled = lax.map(pool_block, (pick_blocks, count_blocks)).reshape(batch_total, emb_width)
    feat_ids = jnp.arange(owner_map.shape[0], dtype=jnp.int32)
    node_ids = jnp.arange(node_count, dtype=jnp.int32)
    source_dev = node_ids * lane_count + my_lane
    source_feat = jnp.sum(
        jnp.where(owner_map[None, :] == source_dev[:, None], feat_ids[None, :], 0), axis=1
    )
    source_group = source_feat // node_count
    same_group = source_group[:, None] == source_group[None, :]
    earlier = node_ids[None, :] < node_ids[:, None]
    source_slot = source_group * capacity + jnp.sum(
        (same_group & earlier).astype(jnp.int32), axis=1
    )
    group_owners = lax.dynamic_slice_in_dim(owner_map, my_lane * node_count, node_count)
    owner_lane = group_owners % lane_count
    owner_node = group_owners // lane_count
    ahead_same = (owner_lane[:, None] == owner_lane[None, :]) & (
        owner_node[None, :] < owner_node[:, None]
    )
    owner_slot = owner_lane * capacity + jnp.sum(ahead_same.astype(jnp.int32), axis=1)
    slot_ids = jnp.arange(slot_total, dtype=jnp.int32)
    zero_bf = jnp.zeros((), jnp.bfloat16)
    outgoing = pooled.reshape(node_count, samples, emb_width)
    arrived = lax.all_to_all(outgoing, "node", split_axis=0, concat_axis=0, tiled=True)
    chosen = source_slot[None, :] == slot_ids[:, None]
    pick_source = jnp.sum(jnp.where(chosen, node_ids[None, :], 0), axis=1)
    filled = jnp.any(chosen, axis=1)
    packed = jnp.where(filled[:, None, None], jnp.take(arrived, pick_source, axis=0), zero_bf)
    landed = lax.all_to_all(
        packed.reshape(lane_count, capacity, samples, emb_width),
        "local",
        split_axis=0,
        concat_axis=0,
        tiled=True,
    )
    x_zero = jnp.take(landed.reshape(slot_total, samples, emb_width), owner_slot, axis=0)
    partial_rank = jnp.einsum("qse,qer->sr", x_zero, cross_down, preferred_element_type=jnp.float32)
    low_rank = lax.psum(partial_rank, "local").astype(jnp.bfloat16)
    cross_term = (
        jnp.einsum("sr,rqe->qse", low_rank, cross_up, preferred_element_type=jnp.float32)
        + cross_bias[:, None, :]
    )
    x_float = x_zero.astype(jnp.float32)
    crossed = (x_float * cross_term + x_float).astype(jnp.bfloat16)
    partial_pre = jnp.einsum("qse,qeh->sh", crossed, mlp_weight, preferred_element_type=jnp.float32)
    share_start = my_lane * share_width
    pre_act = lax.psum(partial_pre, "local") + mlp_bias
    hidden = jax.nn.silu(lax.dynamic_slice_in_dim(pre_act, share_start, share_width, 1)).astype(
        jnp.bfloat16
    )
    sig_pre = jax.nn.sigmoid(pre_act)
    grad_pre = (
        hidden_grad.astype(jnp.float32) * sig_pre * (1.0 + pre_act * (1.0 - sig_pre))
    ).astype(jnp.bfloat16)
    grad_crossed = jnp.einsum(
        "sh,qeh->qse", grad_pre, mlp_weight, preferred_element_type=jnp.float32
    )
    grad_cross = (grad_crossed * x_float).astype(jnp.bfloat16)
    partial_grad_rank = jnp.einsum(
        "qse,rqe->sr", grad_cross, cross_up, preferred_element_type=jnp.float32
    )
    grad_rank = lax.psum(partial_grad_rank.astype(jnp.bfloat16), "local")
    grad_input = (
        grad_crossed * cross_term
        + grad_crossed
        + jnp.einsum("sr,qer->qse", grad_rank, cross_down, preferred_element_type=jnp.float32)
    )
    grad_input = grad_input.astype(jnp.bfloat16)
    back_pick = owner_slot[None, :] == slot_ids[:, None]
    group_ids = jnp.arange(node_count, dtype=jnp.int32)
    back_source = jnp.sum(jnp.where(back_pick, group_ids[None, :], 0), axis=1)
    back_filled = jnp.any(back_pick, axis=1)
    back_packed = jnp.where(
        back_filled[:, None, None], jnp.take(grad_input, back_source, axis=0), zero_bf
    )
    returned = lax.all_to_all(
        back_packed.reshape(lane_count, capacity, samples, emb_width),
        "local",
        split_axis=0,
        concat_axis=0,
        tiled=True,
    )
    by_node = jnp.take(returned.reshape(slot_total, samples, emb_width), source_slot, axis=0)
    home_grad = lax.all_to_all(by_node, "node", split_axis=0, concat_axis=0, tiled=True)

    def add_block(accum, inputs):
        picks, counts, grad_rows = inputs
        matrix = bag_matrix(picks, counts, row_ids)
        update = lax.dot_general(
            matrix, grad_rows, (((0,), (0,)), ((), ())), preferred_element_type=jnp.float32
        )
        return (accum + update, None)

    start_accum = jnp.zeros((rows_here, emb_width), jnp.float32)
    table_grad, unused = lax.scan(add_block, start_accum, (pick_blocks, count_blocks, home_grad))
    return (crossed, hidden, table_grad)


def solution(mesh):
    return jax.shard_map(
        on_device,
        mesh=mesh,
        in_specs=(
            P(),
            P(("node", "local"), None),
            P(("node", "local"), None, None),
            P(("node", "local"), None),
            P("local", None, None),
            P(None, "local", None),
            P("local", None),
            P("local", None, None),
            P(),
            P("node", None),
        ),
        out_specs=(P("local", "node", None), P("node", "local"), P(("node", "local"), None)),
        check_vma=False,
    )
```

profile of v0, /device:TPU:1, one launch (start us, length us, event | category | flops | bytes accessed | tf_op | source)
XLA Modules:
  0.0 739.5 jit_solution(1573936419067823803)
XLA Ops:
  9.3 153.2 %while.24 = (s32[]{:T(128)}, bf16[16,512,128]{2,1,0:T(8,128)(2,1)}, s32[16,512,8]{1,2,0:T(8,128)}, s32[16,512]{1,0:T(8,128)S(1)}, bf16[2048,128]{1,0:T(8,128)(2,1)}, /*index=5*/s32[]{:T(128)}) while((s32[]{:T(128)}, bf16[16,512,128]{2,1,0:T(8,128)(2,1)}, s32[16,512,8]{1,2,0:T(8,128)}, s32[16,512]{1,0:T(8,128)S(1)}, ...), condition=%wide.region_4.5_spmd.clone.clone, body=%wide.region_3.4_spmd.clone.clone.sunk | while | flops 310448128 | bytes 748109 | solution.py:49
  171.8 27.3 %all-to-all-done = bf16[16,512,128]{2,1,0:T(8,128)(2,1)} async-done(((bf16[16,512,128]{2,1,0:T(8,128)(2,1)}), bf16[16,512,128]{2,1,0:T(8,128)(2,1)}, u32[]{:S(2)}, u32[]{:S(2)}) %all-to-all-start) | async-done | bytes 2097184 | tf_op jit(solution)/shard_map/all_to_all | solution.py:72
  220.0 33.0 %all-to-all-done.1 = bf16[8,3,512,128]{3,2,1,0:T(8,128)(2,1)} async-done(((bf16[8,3,512,128]{3,2,1,0:T(8,128)(2,1)}), bf16[8,3,512,128]{3,2,1,0:T(8,128)(2,1)}, u32[]{:S(2)}, u32[]{:S(2)}) %all-to-all-start.1) | async-done | bytes 3145760 | tf_op jit(solution)/shard_map/all_to_all | solution.py:77
  260.9 50.5 %all-reduce.7 = bf16[512,512]{1,0:T(8,128)(2,1)S(1)} all-reduce(f32[512,512]{1,0:T(8,128)} %convolution_bitcast_fusion.1), channel_id=1, replica_groups=mesh['node'=16,'local'=8] {'local'}, use_global_device_ids=true, to_apply=%region_7.10 | all-reduce | flops 262144 | bytes 1572864 | tf_op jit(solution)/shard_map/psum | solution.py:86
  327.0 68.9 %all-reduce.4.cloned.1.call-done = f32[512,2048]{1,0:T(8,128)} async-done(((f32[512,2048]{1,0:T(8,128)}), f32[512,2048]{1,0:T(8,128)}) %all-reduce.4.cloned.1.call-update) | async-done | bytes 4194320 | tf_op jit(solution)/shard_map/psum | solution.py:95
  399.0 11.0 %fusion.117 = f32[512,16,128]{2,0,1:T(8,128)S(1)} fusion(bf16[16,128,2048]{2,1,0:T(8,128)(2,1)} %param.25, f32[512,2048]{1,0:T(8,128)S(1)} %broadcast_add_fusion, bf16[512,2048]{1,0:T(8,128)(2,1)S(1)} %copy-done.9), kind=kOutput, calls=%fused_computation.140 | convolution fusion | flops 4305453056 | bytes 18874368 | tf_op jit(solution)/shard_map/sh,qeh->qse/dot_general | solution.py:103
  414.1 60.6 %all-reduce.6.cloned.1.call-done = bf16[512,512]{1,0:T(8,128)(2,1)} async-done(((bf16[512,512]{1,0:T(8,128)(2,1)}), bf16[512,512]{1,0:T(8,128)(2,1)}) %all-reduce.6.cloned.1.call-update) | async-done | bytes 524304 | tf_op jit(solution)/shard_map/psum | solution.py:110
  496.5 37.7 %all-to-all-done.2 = bf16[8,3,512,128]{3,2,1,0:T(8,128)(2,1)} async-done(((bf16[8,3,512,128]{3,2,1,0:T(8,128)(2,1)}), bf16[8,3,512,128]{3,2,1,0:T(8,128)(2,1)}, u32[]{:S(2)}, u32[]{:S(2)}) %all-to-all-start.2) | async-done | bytes 3145760 | tf_op jit(solution)/shard_map/all_to_all | solution.py:124
  550.1 24.6 %all-to-all-done.3 = bf16[16,512,128]{2,1,0:T(8,128)(2,1)} async-done(((bf16[16,512,128]{2,1,0:T(8,128)(2,1)}), bf16[16,512,128]{2,1,0:T(8,128)(2,1)}, u32[]{:S(2)}, u32[]{:S(2)}) %all-to-all-start.3) | async-done | bytes 2097184 | tf_op jit(solution)/shard_map/all_to_all | solution.py:132
  574.7 157.9 %while.25 = (s32[]{:T(128)}, f32[2048,128]{1,0:T(8,128)}, s32[16,512,8]{1,2,0:T(8,128)}, s32[16,512]{1,0:T(8,128)S(1)}, bf16[16,512,128]{2,1,0:T(8,128)(2,1)}, /*index=5*/s32[]{:T(128)}, s32[]{:T(128)}) while((s32[]{:T(128)}, f32[2048,128]{1,0:T(8,128)}, s32[16,512,8]{1,2,0:T(8,128)}, s32[16,512]{1,0:T(8,128)S(1)}, ...), condition=%wide.region_13.16_spmd.clone.clone, body=%wide.region_12.15_spmd.clone.clone.sunk | while | flops 310906880 | bytes 2320991 | solution.py:143
  585.0 9.1 %convolution_add_fusion.2 = f32[2048,128]{1,0:T(8,128)} fusion(s32[512]{0:T(512)S(1)} %bitcast.118, s32[512]{0:T(512)S(1)} %bitcast.119, s32[512]{0:T(512)S(1)} %bitcast.120, s32[512]{0:T(512)S(1)} %bitcast.121, s32[512]{0:T(512)S(1)} %bitcast.122, s32[512]{0:T(512)S(1)} %bitcast.123, s32[512]{0:T(512)S(1)} %bitcast.124, s32[512]{0:T(512)S(1)} %bitcast.117, ...), kind=kOutput, calls=%fused_computation.91.clone.1 | convolution fusion | flops 310902784 | bytes 2249217 | tf_op jit(solution)/shard_map/while/body/eval_jaxpr/dot_general | solution.py:137
  594.9 9.1 %convolution_add_fusion.2 = f32[2048,128]{1,0:T(8,128)} fusion(s32[512]{0:T(512)S(1)} %bitcast.118, s32[512]{0:T(512)S(1)} %bitcast.119, s32[512]{0:T(512)S(1)} %bitcast.120, s32[512]{0:T(512)S(1)} %bitcast.121, s32[512]{0:T(512)S(1)} %bitcast.122, s32[512]{0:T(512)S(1)} %bitcast.123, s32[512]{0:T(512)S(1)} %bitcast.124, s32[512]{0:T(512)S(1)} %bitcast.117, ...), kind=kOutput, calls=%fused_computation.91.clone.1 | convolution fusion | flops 310902784 | bytes 2249217 | tf_op jit(solution)/shard_map/while/body/eval_jaxpr/dot_general | solution.py:137
  604.8 9.1 %convolution_add_fusion.2 = f32[2048,128]{1,0:T(8,128)} fusion(s32[512]{0:T(512)S(1)} %bitcast.118, s32[512]{0:T(512)S(1)} %bitcast.119, s32[512]{0:T(512)S(1)} %bitcast.120, s32[512]{0:T(512)S(1)} %bitcast.121, s32[512]{0:T(512)S(1)} %bitcast.122, s32[512]{0:T(512)S(1)} %bitcast.123, s32[512]{0:T(512)S(1)} %bitcast.124, s32[512]{0:T(512)S(1)} %bitcast.117, ...), kind=kOutput, calls=%fused_computation.91.clone.1 | convolution fusion | flops 310902784 | bytes 2249217 | tf_op jit(solution)/shard_map/while/body/eval_jaxpr/dot_general | solution.py:137
  614.7 9.1 %convolution_add_fusion.2 = f32[2048,128]{1,0:T(8,128)} fusion(s32[512]{0:T(512)S(1)} %bitcast.118, s32[512]{0:T(512)S(1)} %bitcast.119, s32[512]{0:T(512)S(1)} %bitcast.120, s32[512]{0:T(512)S(1)} %bitcast.121, s32[512]{0:T(512)S(1)} %bitcast.122, s32[512]{0:T(512)S(1)} %bitcast.123, s32[512]{0:T(512)S(1)} %bitcast.124, s32[512]{0:T(512)S(1)} %bitcast.117, ...), kind=kOutput, calls=%fused_computation.91.clone.1 | convolution fusion | flops 310902784 | bytes 2249217 | tf_op jit(solution)/shard_map/while/body/eval_jaxpr/dot_general | solution.py:137
  624.6 9.1 %convolution_add_fusion.2 = f32[2048,128]{1,0:T(8,128)} fusion(s32[512]{0:T(512)S(1)} %bitcast.118, s32[512]{0:T(512)S(1)} %bitcast.119, s32[512]{0:T(512)S(1)} %bitcast.120, s32[512]{0:T(512)S(1)} %bitcast.121, s32[512]{0:T(512)S(1)} %bitcast.122, s32[512]{0:T(512)S(1)} %bitcast.123, s32[512]{0:T(512)S(1)} %bitcast.124, s32[512]{0:T(512)S(1)} %bitcast.117, ...), kind=kOutput, calls=%fused_computation.91.clone.1 | convolution fusion | flops 310902784 | bytes 2249217 | tf_op jit(solution)/shard_map/while/body/eval_jaxpr/dot_general | solution.py:137
  634.5 9.1 %convolution_add_fusion.2 = f32[2048,128]{1,0:T(8,128)} fusion(s32[512]{0:T(512)S(1)} %bitcast.118, s32[512]{0:T(512)S(1)} %bitcast.119, s32[512]{0:T(512)S(1)} %bitcast.120, s32[512]{0:T(512)S(1)} %bitcast.121, s32[512]{0:T(512)S(1)} %bitcast.122, s32[512]{0:T(512)S(1)} %bitcast.123, s32[512]{0:T(512)S(1)} %bitcast.124, s32[512]{0:T(512)S(1)} %bitcast.117, ...), kind=kOutput, calls=%fused_computation.91.clone.1 | convolution fusion | flops 310902784 | bytes 2249217 | tf_op jit(solution)/shard_map/while/body/eval_jaxpr/dot_general | solution.py:137
  644.4 9.1 %convolution_add_fusion.2 = f32[2048,128]{1,0:T(8,128)} fusion(s32[512]{0:T(512)S(1)} %bitcast.118, s32[512]{0:T(512)S(1)} %bitcast.119, s32[512]{0:T(512)S(1)} %bitcast.120, s32[512]{0:T(512)S(1)} %bitcast.121, s32[512]{0:T(512)S(1)} %bitcast.122, s32[512]{0:T(512)S(1)} %bitcast.123, s32[512]{0:T(512)S(1)} %bitcast.124, s32[512]{0:T(512)S(1)} %bitcast.117, ...), kind=kOutput, calls=%fused_computation.91.clone.1 | convolution fusion | flops 310902784 | bytes 2249217 | tf_op jit(solution)/shard_map/while/body/eval_jaxpr/dot_general | solution.py:137
  654.3 9.1 %convolution_add_fusion.2 = f32[2048,128]{1,0:T(8,128)} fusion(s32[512]{0:T(512)S(1)} %bitcast.118, s32[512]{0:T(512)S(1)} %bitcast.119, s32[512]{0:T(512)S(1)} %bitcast.120, s32[512]{0:T(512)S(1)} %bitcast.121, s32[512]{0:T(512)S(1)} %bitcast.122, s32[512]{0:T(512)S(1)} %bitcast.123, s32[512]{0:T(512)S(1)} %bitcast.124, s32[512]{0:T(512)S(1)} %bitcast.117, ...), kind=kOutput, calls=%fused_computation.91.clone.1 | convolution fusion | flops 310902784 | bytes 2249217 | tf_op jit(solution)/shard_map/while/body/eval_jaxpr/dot_general | solution.py:137
  664.2 9.1 %convolution_add_fusion.2 = f32[2048,128]{1,0:T(8,128)} fusion(s32[512]{0:T(512)S(1)} %bitcast.118, s32[512]{0:T(512)S(1)} %bitcast.119, s32[512]{0:T(512)S(1)} %bitcast.120, s32[512]{0:T(512)S(1)} %bitcast.121, s32[512]{0:T(512)S(1)} %bitcast.122, s32[512]{0:T(512)S(1)} %bitcast.123, s32[512]{0:T(512)S(1)} %bitcast.124, s32[512]{0:T(512)S(1)} %bitcast.117, ...), kind=kOutput, calls=%fused_computation.91.clone.1 | convolution fusion | flops 310902784 | bytes 2249217 | tf_op jit(solution)/shard_map/while/body/eval_jaxpr/dot_general | solution.py:137
  674.1 9.1 %convolution_add_fusion.2 = f32[2048,128]{1,0:T(8,128)} fusion(s32[512]{0:T(512)S(1)} %bitcast.118, s32[512]{0:T(512)S(1)} %bitcast.119, s32[512]{0:T(512)S(1)} %bitcast.120, s32[512]{0:T(512)S(1)} %bitcast.121, s32[512]{0:T(512)S(1)} %bitcast.122, s32[512]{0:T(512)S(1)} %bitcast.123, s32[512]{0:T(512)S(1)} %bitcast.124, s32[512]{0:T(512)S(1)} %bitcast.117, ...), kind=kOutput, calls=%fused_computation.91.clone.1 | convolution fusion | flops 310902784 | bytes 2249217 | tf_op jit(solution)/shard_map/while/body/eval_jaxpr/dot_general | solution.py:137
  684.0 9.1 %convolution_add_fusion.2 = f32[2048,128]{1,0:T(8,128)} fusion(s32[512]{0:T(512)S(1)} %bitcast.118, s32[512]{0:T(512)S(1)} %bitcast.119, s32[512]{0:T(512)S(1)} %bitcast.120, s32[512]{0:T(512)S(1)} %bitcast.121, s32[512]{0:T(512)S(1)} %bitcast.122, s32[512]{0:T(512)S(1)} %bitcast.123, s32[512]{0:T(512)S(1)} %bitcast.124, s32[512]{0:T(512)S(1)} %bitcast.117, ...), kind=kOutput, calls=%fused_computation.91.clone.1 | convolution fusion | flops 310902784 | bytes 2249217 | tf_op jit(solution)/shard_map/while/body/eval_jaxpr/dot_general | solution.py:137
  693.9 9.1 %convolution_add_fusion.2 = f32[2048,128]{1,0:T(8,128)} fusion(s32[512]{0:T(512)S(1)} %bitcast.118, s32[512]{0:T(512)S(1)} %bitcast.119, s32[512]{0:T(512)S(1)} %bitcast.120, s32[512]{0:T(512)S(1)} %bitcast.121, s32[512]{0:T(512)S(1)} %bitcast.122, s32[512]{0:T(512)S(1)} %bitcast.123, s32[512]{0:T(512)S(1)} %bitcast.124, s32[512]{0:T(512)S(1)} %bitcast.117, ...), kind=kOutput, calls=%fused_computation.91.clone.1 | convolution fusion | flops 310902784 | bytes 2249217 | tf_op jit(solution)/shard_map/while/body/eval_jaxpr/dot_general | solution.py:137
  703.8 9.1 %convolution_add_fusion.2 = f32[2048,128]{1,0:T(8,128)} fusion(s32[512]{0:T(512)S(1)} %bitcast.118, s32[512]{0:T(512)S(1)} %bitcast.119, s32[512]{0:T(512)S(1)} %bitcast.120, s32[512]{0:T(512)S(1)} %bitcast.121, s32[512]{0:T(512)S(1)} %bitcast.122, s32[512]{0:T(512)S(1)} %bitcast.123, s32[512]{0:T(512)S(1)} %bitcast.124, s32[512]{0:T(512)S(1)} %bitcast.117, ...), kind=kOutput, calls=%fused_computation.91.clone.1 | convolution fusion | flops 310902784 | bytes 2249217 | tf_op jit(solution)/shard_map/while/body/eval_jaxpr/dot_general | solution.py:137
  723.6 9.1 %convolution_add_fusion.2 = f32[2048,128]{1,0:T(8,128)} fusion(s32[512]{0:T(512)S(1)} %bitcast.118, s32[512]{0:T(512)S(1)} %bitcast.119, s32[512]{0:T(512)S(1)} %bitcast.120, s32[512]{0:T(512)S(1)} %bitcast.121, s32[512]{0:T(512)S(1)} %bitcast.122, s32[512]{0:T(512)S(1)} %bitcast.123, s32[512]{0:T(512)S(1)} %bitcast.124, s32[512]{0:T(512)S(1)} %bitcast.117, ...), kind=kOutput, calls=%fused_computation.91.clone.1 | convolution fusion | flops 310902784 | bytes 2249217 | tf_op jit(solution)/shard_map/while/body/eval_jaxpr/dot_general | solution.py:137
  (185 shorter events, 284.2 us)
Async XLA Ops:
  7.2 249.9 %copy-start = (bf16[16,128,512]{2,1,0:T(8,128)(2,1)S(1)}, bf16[16,128,512]{2,1,0:T(8,128)(2,1)}, u32[]{:S(2)}) copy-start(bf16[16,128,512]{2,1,0:T(8,128)(2,1)} %param.22) | copy-start | bytes 6291460
  162.5 8.6 %copy-start.8 = (s32[128]{0:T(128)S(1)}, s32[128]{0:T(128)}, u32[]{:S(2)}) copy-start(s32[128]{0:T(128)} %param.18) | copy-start | bytes 1540
  162.5 36.6 %all-to-all-start = ((bf16[16,512,128]{2,1,0:T(8,128)(2,1)}), bf16[16,512,128]{2,1,0:T(8,128)(2,1)}, u32[]{:S(2)}, u32[]{:S(2)}) async-start(bf16[16,512,128]{2,1,0:T(8,128)(2,1)} %get-tuple-element.111), calls=%async_computation | async-start | bytes 4194304 | tf_op jit(solution)/shard_map/all_to_all | solution.py:72
  207.4 45.6 %all-to-all-start.1 = ((bf16[8,3,512,128]{3,2,1,0:T(8,128)(2,1)}), bf16[8,3,512,128]{3,2,1,0:T(8,128)(2,1)}, u32[]{:S(2)}, u32[]{:S(2)}) async-start(bf16[8,3,512,128]{3,2,1,0:T(8,128)(2,1)} %bitcast.114), calls=%async_computation.1 | async-start | bytes 6291456 | tf_op jit(solution)/shard_map/all_to_all | solution.py:77
  215.3 180.6 %all-reduce.4.cloned.1.call-start = ((), (), s32[]{:S(2)}) async-start(), calls=%async_computation.4 | async-start | bytes 8388608 | tf_op jit(solution)/shard_map/psum | solution.py:95
  257.0 54.4 %copy-start.6 = (f32[16,128]{1,0:T(8,128)S(1)}, f32[16,128]{1,0:T(8,128)}, u32[]{:S(2)}) copy-start(f32[16,128]{1,0:T(8,128)} %param.24) | copy-start | bytes 24580
  317.0 1.3 copy-start.3
  326.5 69.4 %copy-start.7 = (f32[2048]{0:T(1024)S(1)}, f32[2048]{0:T(1024)}, u32[]{:S(2)}) copy-start(f32[2048]{0:T(1024)} %param.26) | copy-start | bytes 24580
  326.5 148.2 %all-reduce.6.cloned.1.call-start = ((), (), s32[]{:S(2)}) async-start(), calls=%async_computation.5 | async-start | bytes 1048576 | tf_op jit(solution)/shard_map/psum | solution.py:110
  395.9 3.0 copy-start.9
  398.9 11.0 %copy-start.4 = (f32[512,2048]{1,0:T(8,128)}, f32[512,2048]{1,0:T(8,128)S(1)}, u32[]{:S(2)}) copy-start(f32[512,2048]{1,0:T(8,128)S(1)} %broadcast_add_fusion) | copy-start | bytes 12582916
  398.9 13.0 %copy-start.1 = (bf16[512,16,128]{0,2,1:T(8,128)(2,1)S(1)}, bf16[512,16,128]{0,2,1:T(8,128)(2,1)}, u32[]{:S(2)}) copy-start(bf16[512,16,128]{0,2,1:T(8,128)(2,1)} %copy.15) | copy-start | bytes 6291460
  399.0 13.0 %copy-start.2 = (bf16[16,512,128]{2,1,0:T(8,128)(2,1)S(1)}, bf16[16,512,128]{2,1,0:T(8,128)(2,1)}, u32[]{:S(2)}) copy-start(bf16[16,512,128]{2,1,0:T(8,128)(2,1)} %gather_fusion.1) | copy-start | bytes 6291460
  410.0 2.0 copy-start.5
  489.4 44.7 %all-to-all-start.2 = ((bf16[8,3,512,128]{3,2,1,0:T(8,128)(2,1)}), bf16[8,3,512,128]{3,2,1,0:T(8,128)(2,1)}, u32[]{:S(2)}, u32[]{:S(2)}) async-start(bf16[8,3,512,128]{3,2,1,0:T(8,128)(2,1)} %bitcast.115), calls=%async_computation.2 | async-start | bytes 6291456 | tf_op jit(solution)/shard_map/all_to_all | solution.py:124
  541.5 33.2 %all-to-all-start.3 = ((bf16[16,512,128]{2,1,0:T(8,128)(2,1)}), bf16[16,512,128]{2,1,0:T(8,128)(2,1)}, u32[]{:S(2)}, u32[]{:S(2)}) async-start(bf16[16,512,128]{2,1,0:T(8,128)(2,1)} %broadcast_select_fusion), calls=%async_computation.3 | async-start | bytes 4194304 | tf_op jit(solution)/shard_map/all_to_all | solution.py:132
Sparse Core Ops, SparseCore 0:
  326.7 69.1 all-reduce.3
  414.2 60.4 all-reduce.5
where the time goes:
time: 747 us; the launch traced here: 739 us
  matrix products  322 us (43%)
  waiting for transfers between devices  252 us (34%)
  blocking collectives  50.5 us (7%)
  local copies, waits for them, and re-layouts  48.5 us (6%)
  starting transfers between devices  30.5 us (4%)
  other arithmetic  21.1 us (3%)
  between operations  14.2 us (2%)
    dot_general x16, matrix products, add_block(): lax.dot_general(matrix, grad_rows, (((0,), (0,)), ((), ())), preferred_el...  145 us
    dot_general x16, matrix products, pool_block(): jnp.dot(matrix, tables, preferred_element_type=jnp.float32)  140 us
    psum x1, waiting for transfers between devices, on_device(): pre_act = lax.psum(partial_pre, 'local') + mlp_bias  68.9 us
    psum x1, waiting for transfers between devices, on_device(): grad_rank = lax.psum(partial_grad_rank.astype(jnp.bfloat16), 'local')  60.6 us
    psum x1, blocking collectives, on_device(): low_rank = lax.psum(partial_rank, 'local').astype(jnp.bfloat16)  50.5 us
    all_to_all x1, waiting for transfers between devices, on_device(): lax.all_to_all(back_packed.reshape(lane_count, capacity, samples, emb_wid...  37.7 us
    all_to_all x1, waiting for transfers between devices, on_device(): lax.all_to_all(packed.reshape(lane_count, capacity, samples, emb_width),...  33 us
    all_to_all x1, waiting for transfers between devices, on_device(): lax.all_to_all(outgoing, 'node', split_axis=0, concat_axis=0, tiled=True)  27.3 us
  transfers between devices with their start and end apart: 6, of which 6 were waited for; matrix products, arithmetic and copies ran while one was open for 1% of the time, Pallas kernels for 0%

commit v1 on v0

v1 whole, which is shorter than its diff:
```python
import functools

import jax
import jax.numpy as jnp
from jax import lax
from jax.experimental import pallas as pl
from jax.experimental.pallas import tpu as pltpu
from jax.sharding import PartitionSpec as P

BF = jnp.bfloat16
F32 = jnp.float32
MESH = pl.DeviceIdType.MESH
PIECES = 4
BAG_GROUP = 32
LOW = 256


def dot(a, b, contract=((1,), (0,))):
    return lax.dot_general(a, b, (contract, ((), ())), preferred_element_type=F32)


def greet(n_node, n_local, node, lane):
    barrier = pltpu.get_barrier_semaphore()

    def by_node(k, carry):
        peer = lax.rem(node + k, n_node)
        pl.semaphore_signal(barrier, inc=1, device_id=(peer, lane), device_id_type=MESH)
        return carry

    def by_lane(d, carry):
        peer = lax.rem(lane + d, n_local)
        pl.semaphore_signal(barrier, inc=1, device_id=(node, peer), device_id_type=MESH)
        return carry

    lax.fori_loop(1, n_node, by_node, 0)
    lax.fori_loop(1, n_local, by_lane, 0)
    pl.semaphore_wait(barrier, n_node + n_local - 2)


def flatten_picks(idx_ref, size_ref, iota_ref, key_ref, low_ref):
    iota_ref[...] = lax.broadcasted_iota(jnp.int32, iota_ref.shape, 0).astype(F32).astype(BF)
    lanes = lax.broadcasted_iota(jnp.int32, (1, 128), 1)
    depth = lax.broadcasted_iota(jnp.int32, (8, 128), 0)

    def eight_groups(b, carry):
        rows = [[], []]
        for half in range(2):
            off = pl.multiple_of(b * 256 + half * 128, 128)
            picks = jnp.where(depth < size_ref[:, pl.ds(off, 128)], idx_ref[:, pl.ds(off, 128)], -1)
            turned = [picks] + [pltpu.roll(picks, 32 * d, 1) for d in (1, 2, 3)]
            for group in range(4):
                for h in range(2):
                    row = turned[(3 - group) % 4][4 * h + 3 : 4 * h + 4]
                    for q in (2, 1, 0):
                        source = turned[(q - group) % 4][4 * h + q : 4 * h + q + 1]
                        row = jnp.where(lanes < 32 * (q + 1), source, row)
                    rows[h].append(row)
        here = pl.ds(pl.multiple_of(b * 8, 8), 8)
        for h in range(2):
            picks = jnp.concatenate(rows[h], 0)
            key_ref[here, h * 128 : (h + 1) * 128] = ((picks >> 8) * 32 + (lanes & 31)).astype(F32)
            low_ref[here, h * 128 : (h + 1) * 128] = (picks & 255).astype(F32)
        return carry

    lax.fori_loop(0, idx_ref.shape[1] // 256, eight_groups, 0)


def count_group(key_ref, low_ref, iota_ref, group):
    iota = iota_ref[...]
    one, zero = jnp.ones((), BF), jnp.zeros((), BF)
    hot = []
    for ref in (key_ref, low_ref):
        row = jnp.broadcast_to(ref[pl.ds(group, 1), :], (16, LOW)).astype(BF)
        hot.append(jnp.where(jnp.concatenate([row] * 16, 0) == iota, one, zero))
    return dot(hot[0], hot[1], ((1,), (1,))).astype(BF)


def put_counts(count_ref, where, row, counts):
    for h in range(8):
        columns = slice(h * LOW, (h + 1) * LOW)
        if where is None:
            count_ref[pl.ds(row, BAG_GROUP), columns] = counts[h * 32 : (h + 1) * 32]
        else:
            count_ref[where, pl.ds(row, BAG_GROUP), columns] = counts[h * 32 : (h + 1) * 32]


def pool_kernel(
    n_node, n_local, pick_ref, slot_ref, idx_ref, size_ref, table_ref, x_ref,
    iota, key, low, counts, pooled, packed, node_send, node_recv, lane_send, lane_recv, *places,
):
    node, lane = lax.axis_index("node"), lax.axis_index("local")
    arrived, landed = places[:PIECES], places[PIECES:]
    cap = packed.shape[2]
    rows = pooled.shape[2]
    per_node = PIECES * rows // BAG_GROUP
    greet(n_node, n_local, node, lane)
    flatten_picks(idx_ref, size_ref, iota, key, low)

    def to_node(p, k):
        return pltpu.make_async_remote_copy(
            src_ref=pooled.at[p, k],
            dst_ref=arrived[p].at[node],
            send_sem=node_send.at[p, k],
            recv_sem=node_recv.at[p, k],
            device_id=(lax.rem(node + k, n_node), lane),
            device_id_type=MESH,
        )

    def to_lane(p, d):
        return pltpu.make_async_remote_copy(
            src_ref=packed.at[p, d],
            dst_ref=landed[p].at[pl.ds(lane * cap, cap)],
            send_sem=lane_send.at[p, d],
            recv_sem=lane_recv.at[p, d],
            device_id=(node, lax.rem(lane + d, n_local)),
            device_id_type=MESH,
        )

    def pool_piece(p):
        def four_nodes(c, carry):
            for i in range(16):
                source = lax.rem(node + c * 4 + i // 4, n_node)
                group = source * per_node + p * 4 + i % 4
                put_counts(counts, None, i * BAG_GROUP, count_group(key, low, iota, group))
            sums = dot(counts[...], table_ref[...]).astype(BF)
            for i in range(4):
                pooled[p, c * 4 + i] = sums[i * rows : (i + 1) * rows]

            for piece in range(PIECES):

                @pl.when(p == piece)
                def _():
                    def send(k, inner):
                        to_node(piece, k).start()
                        return inner

                    lax.fori_loop(jnp.maximum(c * 4, 1), c * 4 + 4, send, 0)

            return carry

        lax.fori_loop(0, n_node // 4, four_nodes, 0)

    def pack_piece(p):
        def arrive(k, carry):
            to_node(p, k).wait_recv()
            return carry

        lax.fori_loop(1, n_node, arrive, 0)
        arrived[p][node] = pooled[p, 0]
        for c in range(cap):
            landed[p][lane * cap + c] = arrived[p][pick_ref[lane * cap + c]]

        def send(d, carry):
            target = lax.rem(lane + d, n_local)
            for c in range(cap):
                packed[p, d, c] = arrived[p][pick_ref[target * cap + c]]
            to_lane(p, d).start()
            return carry

        lax.fori_loop(1, n_local, send, 0)

    def unpack_piece(p):
        def land(d, carry):
            to_lane(p, d).wait_recv()
            return carry

        lax.fori_loop(1, n_local, land, 0)
        for q in range(n_node):
            x_ref[p * rows : (p + 1) * rows, q * 128 : (q + 1) * 128] = landed[p][slot_ref[q]]

    def turn(p, carry):
        pool_piece(p)
        for piece in range(PIECES - 1):

            @pl.when(p == piece + 1)
            def _():
                pack_piece(piece)

        return carry

    lax.fori_loop(0, PIECES, turn, 0)
    pack_piece(PIECES - 1)

    for p in range(PIECES):
        unpack_piece(p)

        def sent_node(k, inner):
            to_node(p, k).wait_send()
            return inner

        def sent_lane(d, inner):
            to_lane(p, d).wait_send()
            return inner

        lax.fori_loop(1, n_node, sent_node, 0)
        lax.fori_loop(1, n_local, sent_lane, 0)


def scatter_kernel(
    n_node, n_local, pick_ref, slot_ref, idx_ref, size_ref, grad_ref, out_ref,
    iota, key, low, counts, packed, routed, home, home_t, total, lane_send, lane_recv, node_send, node_recv, *landed,
):
    node, lane = lax.axis_index("node"), lax.axis_index("local")
    cap = packed.shape[2]
    rows = packed.shape[3]
    per_node = PIECES * rows // BAG_GROUP
    greet(n_node, n_local, node, lane)

    def to_lane(p, d):
        return pltpu.make_async_remote_copy(
            src_ref=packed.at[p, d],
            dst_ref=landed[p].at[pl.ds(lane * cap, cap)],
            send_sem=lane_send.at[p, d],
            recv_sem=lane_recv.at[p, d],
            device_id=(node, lax.rem(lane + d, n_local)),
            device_id_type=MESH,
        )

    def to_node(p, k):
        return pltpu.make_async_remote_copy(
            src_ref=routed.at[p, k],
            dst_ref=home.at[p, node],
            send_sem=node_send.at[p, k],
            recv_sem=node_recv.at[p, k],
            device_id=(lax.rem(node + k, n_node), lane),
            device_id_type=MESH,
        )

    def pack_piece(p):
        here = slice(p * rows, (p + 1) * rows)

        def send(d, inner):
            target = lax.rem(lane + d, n_local)
            for c in range(cap):
                packed[p, d, c] = grad_ref[pick_ref[target * cap + c], here]
            to_lane(p, d).start()
            return inner

        lax.fori_loop(1, n_local, send, 0)
        for c in range(cap):
            landed[p][lane * cap + c] = grad_ref[pick_ref[lane * cap + c], here]

    def count_piece(p):
        def four_nodes(c, carry):
            for i in range(16):
                group = (c * 4 + i // 4) * per_node + p * 4 + i % 4
                row = pl.multiple_of(c * 16 * BAG_GROUP + i * BAG_GROUP, BAG_GROUP)
                put_counts(counts, p, row, count_group(key, low, iota, group))
            return carry

        lax.fori_loop(0, n_node // 4, four_nodes, 0)

    def route_piece(p):
        def land(d, carry):
            to_lane(p, d).wait_recv()
            return carry

        lax.fori_loop(1, n_local, land, 0)

        def send(k, carry):
            routed[p, k] = landed[p][slot_ref[lax.rem(node + k, n_node)]]
            to_node(p, k).start()
            return carry

        lax.fori_loop(1, n_node, send, 0)
        home[p, node] = landed[p][slot_ref[node]]

    def add_piece(p):
        def arrive(k, carry):
            to_node(p, k).wait_recv()
            return carry

        lax.fori_loop(1, n_node, arrive, 0)
        for n in range(n_node):
            home_t[:, n * rows : (n + 1) * rows] = home[p, n].T

        def columns(c, carry):
            here = pl.ds(pl.multiple_of(c * 512, 512), 512)
            total[:, here] += dot(home_t[...], counts[p, :, here])
            return carry

        lax.fori_loop(0, total.shape[1] // 512, columns, 0)

    for p in range(PIECES):
        pack_piece(p)
    flatten_picks(idx_ref, size_ref, iota, key, low)
    total[...] = jnp.zeros_like(total)

    def turn(p, carry):
        @pl.when(p < PIECES)
        def _():
            count_piece(p)

        for piece in range(PIECES):

            @pl.when(p == piece + 2)
            def _():
                route_piece(piece)

        @pl.when(p >= 3)
        def _():
            add_piece(p - 3)

        return carry

    lax.fori_loop(0, PIECES + 3, turn, 0)
    for n in range(total.shape[1] // 128):
        out_ref[n * 128 : (n + 1) * 128, :] = total[:, n * 128 : (n + 1) * 128].T

    for p in range(PIECES):

        def sent_node(k, inner):
            to_node(p, k).wait_send()
            return inner

        def sent_lane(d, inner):
            to_lane(p, d).wait_send()
            return inner

        lax.fori_loop(1, n_node, sent_node, 0)
        lax.fori_loop(1, n_local, sent_lane, 0)


SMEM = pl.BlockSpec(memory_space=pltpu.SMEM)
VMEM = pl.BlockSpec(memory_space=pltpu.VMEM)
SEM = pltpu.SemaphoreType.DMA


def pool_and_send(pick, slot, picks, sizes, tables, n_node, n_local, cap, samples):
    rows = samples // PIECES
    groups = picks.shape[1] // BAG_GROUP
    width = tables.shape[1]
    return pl.pallas_call(
        functools.partial(pool_kernel, n_node, n_local),
        out_shape=jax.ShapeDtypeStruct((samples, n_node * width), BF),
        in_specs=[SMEM, SMEM, VMEM, VMEM, VMEM],
        out_specs=VMEM,
        scratch_shapes=[
            pltpu.VMEM((LOW, LOW), BF),
            pltpu.VMEM((groups, LOW), F32),
            pltpu.VMEM((groups, LOW), F32),
            pltpu.VMEM((16 * BAG_GROUP, tables.shape[0]), BF),
            pltpu.VMEM((PIECES, n_node, rows, width), BF),
            pltpu.VMEM((PIECES, n_local, cap, rows, width), BF),
            SEM((PIECES, n_node)),
            SEM((PIECES, n_node)),
            SEM((PIECES, n_local)),
            SEM((PIECES, n_local)),
            *[pltpu.VMEM((n_node, rows, width), BF)] * PIECES,
            *[pltpu.VMEM((n_local * cap, rows, width), BF)] * PIECES,
        ],
        compiler_params=pltpu.CompilerParams(collective_id=0, has_side_effects=True, vmem_limit_bytes=48 << 20),
        name="pool_and_send",
    )(pick, slot, picks, sizes, tables)


def send_and_scatter(pick, slot, picks, sizes, grads, table_rows, n_node, n_local, cap):
    samples, width = grads.shape[1:]
    rows = samples // PIECES
    groups = picks.shape[1] // BAG_GROUP
    return pl.pallas_call(
        functools.partial(scatter_kernel, n_node, n_local),
        out_shape=jax.ShapeDtypeStruct((table_rows, width), F32),
        in_specs=[SMEM, SMEM, VMEM, VMEM, VMEM],
        out_specs=VMEM,
        scratch_shapes=[
            pltpu.VMEM((LOW, LOW), BF),
            pltpu.VMEM((groups, LOW), F32),
            pltpu.VMEM((groups, LOW), F32),
            pltpu.VMEM((PIECES, n_node * rows, table_rows), BF),
            pltpu.VMEM((PIECES, n_local, cap, rows, width), BF),
            pltpu.VMEM((PIECES, n_node, rows, width), BF),
            pltpu.VMEM((PIECES, n_node, rows, width), BF),
            pltpu.VMEM((width, n_node * rows), BF),
            pltpu.VMEM((width, table_rows), F32),
            SEM((PIECES, n_local)),
            SEM((PIECES, n_local)),
            SEM((PIECES, n_node)),
            SEM((PIECES, n_node)),
            *[pltpu.VMEM((n_local * cap, rows, width), BF)] * PIECES,
        ],
        compiler_params=pltpu.CompilerParams(collective_id=1, has_side_effects=True, vmem_limit_bytes=56 << 20),
        name="send_and_scatter",
    )(pick, slot, picks, sizes, grads)


def on_device(
    owner_map,
    bag_sizes,
    indices,
    tables,
    cross_down,
    cross_up,
    cross_bias,
    mlp_weight,
    mlp_bias,
    hidden_grad,
):
    node_count = lax.axis_size("node")
    lane_count = lax.axis_size("local")
    my_lane = lax.axis_index("local")
    capacity = node_count // lane_count + 1
    slot_total = lane_count * capacity
    samples = hidden_grad.shape[0]
    emb_width = tables.shape[1]
    hidden_width = hidden_grad.shape[1]
    share_width = hidden_width // lane_count
    picks = indices[0].T
    feat_ids = jnp.arange(owner_map.shape[0], dtype=jnp.int32)
    node_ids = jnp.arange(node_count, dtype=jnp.int32)
    source_dev = node_ids * lane_count + my_lane
    source_feat = jnp.sum(
        jnp.where(owner_map[None, :] == source_dev[:, None], feat_ids[None, :], 0), axis=1
    )
    source_group = source_feat // node_count
    same_group = source_group[:, None] == source_group[None, :]
    earlier = node_ids[None, :] < node_ids[:, None]
    source_slot = source_group * capacity + jnp.sum(
        (same_group & earlier).astype(jnp.int32), axis=1
    )
    group_owners = lax.dynamic_slice_in_dim(owner_map, my_lane * node_count, node_count)
    owner_lane = group_owners % lane_count
    owner_node = group_owners // lane_count
    ahead_same = (owner_lane[:, None] == owner_lane[None, :]) & (
        owner_node[None, :] < owner_node[:, None]
    )
    owner_slot = owner_lane * capacity + jnp.sum(ahead_same.astype(jnp.int32), axis=1)
    slot_ids = jnp.arange(slot_total, dtype=jnp.int32)
    pick_source = jnp.sum(
        jnp.where(source_slot[None, :] == slot_ids[:, None], node_ids[None, :], 0), axis=1
    )
    back_source = jnp.sum(
        jnp.where(owner_slot[None, :] == slot_ids[:, None], node_ids[None, :], 0), axis=1
    )

    x_zero = pool_and_send(
        pick_source, owner_slot, picks, bag_sizes, tables, node_count, lane_count, capacity, samples
    )
    down = cross_down.reshape(-1, cross_down.shape[2])
    up = cross_up.reshape(cross_up.shape[0], -1)
    weight = mlp_weight.reshape(-1, hidden_width)
    partial_rank = dot(x_zero, down)
    low_rank = lax.psum(partial_rank, "local").astype(BF)
    cross_term = dot(low_rank, up) + cross_bias.reshape(1, -1)
    x_float = x_zero.astype(F32)
    crossed = (x_float * cross_term + x_float).astype(BF)
    partial_pre = dot(crossed, weight)
    share_start = my_lane * share_width
    pre_act = lax.psum(partial_pre, "local") + mlp_bias
    hidden = jax.nn.silu(lax.dynamic_slice_in_dim(pre_act, share_start, share_width, 1)).astype(BF)
    sig_pre = jax.nn.sigmoid(pre_act)
    grad_pre = (hidden_grad.astype(F32) * sig_pre * (1.0 + pre_act * (1.0 - sig_pre))).astype(BF)
    grad_crossed = dot(grad_pre, weight, ((1,), (1,)))
    grad_cross = (grad_crossed * x_float).astype(BF)
    partial_grad_rank = dot(grad_cross, up, ((1,), (1,)))
    grad_rank = lax.psum(partial_grad_rank.astype(BF), "local")
    grad_input = grad_crossed * cross_term + grad_crossed + dot(grad_rank, down, ((1,), (1,)))
    grad_input = grad_input.astype(BF).reshape(samples, node_count, emb_width).transpose(1, 0, 2)
    table_grad = send_and_scatter(
        back_source,
        source_slot,
        picks,
        bag_sizes,
        grad_input,
        tables.shape[0],
        node_count,
        lane_count,
        capacity,
    )
    crossed = crossed.reshape(samples, node_count, emb_width).transpose(1, 0, 2)
    return (crossed, hidden, table_grad)


def solution(mesh):
    return jax.shard_map(
        on_device,
        mesh=mesh,
        in_specs=(
            P(),
            P(("node", "local"), None),
            P(("node", "local"), None, None),
            P(("node", "local"), None),
            P("local", None, None),
            P(None, "local", None),
            P("local", None),
            P("local", None, None),
            P(),
            P("node", None),
        ),
        out_specs=(P("local", "node", None), P("node", "local"), P(("node", "local"), None)),
        check_vma=False,
    )
```

time: 747 us -> 377 us (0.50)
  matrix products: 322 us -> 36.6 us
  waiting for transfers between devices: 252 us -> 126 us
  Pallas kernels: 0 us -> 120 us
  starting transfers between devices: 30.5 us -> 0.26 us
  local copies, waits for them, and re-layouts: 48.5 us -> 21.1 us
  other arithmetic: 21.1 us -> 8.21 us
    dot_general x38 -> x6, matrix products: 322 us -> 36.6 us  [dot(): lax.dot_general(a, b, (contract, ((), ())), preferred_element_type=F32)]
    all_to_all x4 -> x0, waiting for transfers between devices: 123 us -> none  [the longest x1 37.7 us: on_device(): lax.all_to_all(back_packed.reshape(lane_count, capacity, samples, emb_wid...]
    pallas_call x0 -> x2, Pallas kernels: none -> 120 us  [the longest x1 62.2 us: pool_and_send(): pl.pallas_call(functools.partial(pool_kernel, n_node, n_local), out_shape...]
    all_to_all x4 -> x0, starting transfers between devices: 30.3 us -> none  [the longest x1 8.61 us: on_device(): lax.all_to_all(outgoing, 'node', split_axis=0, concat_axis=0, tiled=True)]
    squeeze x32 -> x0, local copies, waits for them, and re-layouts: 23 us -> none  [on_device(): lax.map(pool_block, (pick_blocks, count_blocks))]
    gather x4 -> x0, local copies, waits for them, and re-layouts: 16.8 us -> none  [the longest x1 4.36 us: on_device(): jnp.take(grad_input, back_source, axis=0)]
    select_n x7 -> x0, other arithmetic: 11.3 us -> none  [the longest x1 4.03 us: on_device(): jnp.where(back_filled[:, None, None], jnp.take(grad_input, back_source, a...]
  transfers between devices with their start and end apart: 6 -> 2, of which waited for: 6 -> 2; matrix products, arithmetic and copies ran while one was open for 1% -> 2% of each run, Pallas kernels for 0% -> 0%
where the time goes in v1:
time: 377 us; the launch traced here: 376 us
  waiting for transfers between devices  126 us (33%)
  Pallas kernels  120 us (32%)
  blocking collectives  49.3 us (13%)
  matrix products  36.6 us (10%)
  local copies, waits for them, and re-layouts  21.1 us (6%)
  between operations  14.2 us (4%)
  other arithmetic  8.21 us (2%)
    psum x1, waiting for transfers between devices, on_device(): pre_act = lax.psum(partial_pre, 'local') + mlp_bias  71.3 us
    pallas_call x1, Pallas kernels, pool_and_send(): pl.pallas_call(functools.partial(pool_kernel, n_node, n_local), out_shape...  62.2 us
    pallas_call x1, Pallas kernels, send_and_scatter(): pl.pallas_call(functools.partial(scatter_kernel, n_node, n_local), out_sh...  58 us
    psum x1, waiting for transfers between devices, on_device(): grad_rank = lax.psum(partial_grad_rank.astype(BF), 'local')  54.7 us
    psum x1, blocking collectives, on_device(): low_rank = lax.psum(partial_rank, 'local').astype(BF)  49.3 us
    dot_general x6, matrix products, dot(): lax.dot_general(a, b, (contract, ((), ())), preferred_element_type=F32)  36.6 us
    unnamed x29, local copies, waits for them, and re-layouts  9.76 us
  transfers between devices with their start and end apart: 2, of which 2 were waited for; matrix products, arithmetic and copies ran while one was open for 2% of the time, Pallas kernels for 0%

profile of v1, /device:TPU:1, one launch (start us, length us, event | category | flops | bytes accessed | tf_op | source)
XLA Modules:
  0.0 375.8 jit_solution(14861557120246489481)
XLA Ops:
  7.2 1.0 select_reduce_fusion.2
  10.2 0.9 copy-done.3
  11.1 1.0 copy-done.4
  12.2 0.8 copy-done.5
  12.9 62.2 %pool_and_send.1 = bf16[512,2048]{1,0:T(8,128)(2,1)S(1)} custom-call(s32[24]{0:T(128)S(1)} %select_reduce_fusion.1.pick_ref, s32[16]{0:T(128)S(1)} %multiply_add_fusion.2.slot_ref, s32[8,8192]{1,0:T(8,128)S(1)} %bitcast.36, s32[1,8192]{1,0:T(1,128)S(1)} %copy-done.5, bf16[2048,128]{1,0:T(8,128)(2,1)S(1)} %copy-done.4), custom_call_target="tpu_custom_call" | custom-call | tf_op jit(solution)/shard_map/pool_and_send/pallas_call | solution.py:333
  75.2 1.3 copy-done.1
  76.5 2.2 fusion.21
  78.7 49.3 %all-reduce.7 = bf16[512,512]{1,0:T(8,128)(2,1)S(1)} all-reduce(f32[512,512]{1,0:T(8,128)} %fusion.21), channel_id=1, replica_groups=mesh['node'=16,'local'=8] {'local'}, use_global_device_ids=true, to_apply=%region_4.5 | all-reduce | flops 262144 | bytes 1572864 | tf_op jit(solution)/shard_map/psum | solution.py:443
  128.0 5.6 %fusion.1 = (bf16[512,2048]{1,0:T(8,128)(2,1)S(1)}, f32[512,2048]{1,0:T(8,128)}) fusion(bf16[512,2048]{1,0:T(8,128)(2,1)} %copy-done.1, f32[2048]{0:T(1024)S(1)} %bitcast.41, bf16[512,512]{1,0:T(8,128)(2,1)S(1)} %all-reduce.7, bf16[64,8,16,128]{3,2,1,0:T(8,128)(2,1)} %bitcast.38), kind=kOutput, calls=%fused_computation.4 | convolution fusion | flops 1078984704 | bytes 11018240 | tf_op jit(solution)/shard_map/dot_general | solution.py:19
  133.6 1.4 copy-done.8
  135.0 9.3 %fusion.22 = f32[512,2048]{1,0:T(8,128)} fusion(bf16[512,2048]{1,0:T(8,128)(2,1)S(1)} %get-tuple-element.5, bf16[2048,2048]{1,0:T(8,128)(2,1)} %bitcast.43), kind=kOutput, calls=%fused_computation.44 | convolution fusion | flops 4294967296 | bytes 14680064 | tf_op jit(solution)/shard_map/dot_general | solution.py:19
  144.6 71.3 %all-reduce.4.cloned.1.call-done = f32[512,2048]{1,0:T(8,128)} async-done(((f32[512,2048]{1,0:T(8,128)}), f32[512,2048]{1,0:T(8,128)}) %all-reduce.4.cloned.1.call-update) | async-done | bytes 4194320 | tf_op jit(solution)/shard_map/psum | solution.py:449
  215.9 2.8 broadcast_add_fusion
  218.8 11.0 %fusion.4 = f32[512,2048]{1,0:T(8,128)S(1)} fusion(bf16[2048,2048]{1,0:T(8,128)(2,1)} %bitcast.44, f32[512,2048]{1,0:T(8,128)S(1)} %broadcast_add_fusion, bf16[512,2048]{1,0:T(8,128)(2,1)S(1)} %copy-done.13), kind=kOutput, calls=%fused_computation.8 | convolution fusion | flops 4305453056 | bytes 18874368 | tf_op jit(solution)/shard_map/dot_general | solution.py:19
  229.8 2.0 copy-done.6
  231.8 2.1 fusion.13
  233.9 3.5 bitcast_bitcast_fusion
  238.0 1.9 multiply_convert_fusion.2
  239.9 54.7 %all-reduce.6.cloned.1.call-done = bf16[512,512]{1,0:T(8,128)(2,1)} async-done(((bf16[512,512]{1,0:T(8,128)(2,1)}), bf16[512,512]{1,0:T(8,128)(2,1)}) %all-reduce.6.cloned.1.call-update) | async-done | bytes 524304 | tf_op jit(solution)/shard_map/psum | solution.py:456
  294.5 6.3 %fusion.3 = bf16[512,2048]{1,0:T(8,128)(2,1)} fusion(f32[512,2048]{1,0:T(8,128)} %copy-done.6, f32[512,2048]{1,0:T(8,128)} %get-tuple-element.6, bf16[512,512]{1,0:T(8,128)(2,1)} %all-reduce.6.cloned.1.call-done, bf16[2048,512]{1,0:T(8,128)(2,1)S(1)} %bitcast.34, f32[2048]{0:T(1024)S(1)} %bitcast.42), kind=kOutput, calls=%fused_computation.6 | convolution fusion | flops 1078984704 | bytes 13115392 | tf_op jit(solution)/shard_map/dot_general | solution.py:19
  300.9 3.9 %copy.18 = bf16[512,2048]{0,1:T(8,128)(2,1)} copy(bf16[512,2048]{1,0:T(8,128)(2,1)} %fusion.3) | data formatting | bytes 4194304 | tf_op jit(solution)/shard_map/convert_element_type | solution.py:458
  304.8 3.9 %copy.19 = bf16[512,16,128]{2,0,1:T(8,128)(2,1)} copy(bf16[512,16,128]{0,2,1:T(8,128)(2,1)} %bitcast.40) | data formatting | bytes 4194304 | tf_op jit(solution)/shard_map/reshape | solution.py:458
  308.7 58.0 %send_and_scatter.1 = f32[2048,128]{1,0:T(8,128)} custom-call(s32[24]{0:T(128)} %select_reduce_fusion.pick_ref, s32[16]{0:T(128)} %copy-done.12, s32[8,8192]{1,0:T(8,128)} %bitcast.35, s32[1,8192]{1,0:T(1,128)} %size_ref.3, bf16[16,512,128]{2,1,0:T(8,128)(2,1)} %bitcast.37), custom_call_target="tpu_custom_call" | custom-call | tf_op jit(solution)/shard_map/send_and_scatter/pallas_call | solution.py:361
  366.7 2.3 copy.40
  (36 shorter events, 3.0 us)
Async XLA Ops:
  7.2 68.0 %copy-start = (bf16[16,128,512]{2,1,0:T(8,128)(2,1)S(1)}, bf16[16,128,512]{2,1,0:T(8,128)(2,1)}, u32[]{:S(2)}) copy-start(bf16[16,128,512]{2,1,0:T(8,128)(2,1)} %param.14) | copy-start | bytes 6291460
  7.2 208.7 %all-reduce.4.cloned.1.call-start = ((), (), s32[]{:S(2)}) async-start(), calls=%async_computation | async-start | bytes 8388608 | tf_op jit(solution)/shard_map/psum | solution.py:449
  8.4 70.3 %copy-start.12 = (s32[16]{0:T(128)}, s32[16]{0:T(128)S(1)}, u32[]{:S(2)}) copy-start(s32[16]{0:T(128)S(1)} %multiply_add_fusion.3.slot_ref) | copy-start | bytes 196
  10.2 1.0 copy-start.3
  11.1 1.0 copy-start.4
  12.2 0.8 copy-start.5
  75.2 1.3 copy-start.1
  76.5 51.5 %copy-start.10 = (f32[16,128]{1,0:T(8,128)S(1)}, f32[16,128]{1,0:T(8,128)}, u32[]{:S(2)}) copy-start(f32[16,128]{1,0:T(8,128)} %param.16) | copy-start | bytes 24580
  133.6 1.4 copy-start.8
  144.3 71.6 %copy-start.11 = (f32[2048]{0:T(1024)S(1)}, f32[2048]{0:T(1024)}, u32[]{:S(2)}) copy-start(f32[2048]{0:T(1024)} %param.18) | copy-start | bytes 24580
  144.4 150.2 %all-reduce.6.cloned.1.call-start = ((), (), s32[]{:S(2)}) async-start(), calls=%async_computation.1 | async-start | bytes 1048576 | tf_op jit(solution)/shard_map/psum | solution.py:456
  215.9 2.9 copy-start.13
  218.8 11.0 %copy-start.9 = (f32[512,2048]{1,0:T(8,128)}, f32[512,2048]{1,0:T(8,128)S(1)}, u32[]{:S(2)}) copy-start(f32[512,2048]{1,0:T(8,128)S(1)} %broadcast_add_fusion) | copy-start | bytes 12582916
  218.8 13.0 %copy-start.2 = (bf16[512,2048]{1,0:T(8,128)(2,1)S(1)}, bf16[512,2048]{1,0:T(8,128)(2,1)}, u32[]{:S(2)}) copy-start(bf16[512,2048]{1,0:T(8,128)(2,1)} %copy-done.1) | copy-start | bytes 6291460
  218.8 13.0 %copy-start.7 = (bf16[512,16,128]{2,1,0:T(8,128)(2,1)S(1)}, bf16[512,16,128]{2,1,0:T(8,128)(2,1)}, u32[]{:S(2)}) copy-start(bf16[512,16,128]{2,1,0:T(8,128)(2,1)} %param.15) | copy-start | bytes 6291460
  229.8 2.0 copy-start.6
Sparse Core Ops, SparseCore 0:
  144.5 71.3 all-reduce.3
  234.0 60.4 all-reduce.5

commit v2 on v1

--- a/solution.py
+++ b/solution.py
@@ -11,6 +11,7 @@
 F32 = jnp.float32
 MESH = pl.DeviceIdType.MESH
 PIECES = 4
+HALVES = 2
 BAG_GROUP = 32
 LOW = 256
 
@@ -321,9 +322,239 @@
         lax.fori_loop(1, n_local, sent_lane, 0)
 
 
+def layer_kernel(
+    n_local, x_ref, bias_ref, hbias_ref, grad_hbm, down_hbm, up_hbm, weight_hbm, crossed_ref, hidden_ref, gx_ref,
+    down, up, weight, hgrad, term, gcross, inner, rank_send, rank_recv, rank, sib_send, sib_recv, pre_send, pre_recv,
+    pre_own, gpre, load_sem, rank_ss, rank_rs, share_ss, share_rs, sib_ss, sib_rs, pre_ss, pre_rs, gp_ss, gp_rs,
+    fw_ss, fw_rs,
+):
+    node, lane = lax.axis_index("node"), lax.axis_index("local")
+    chips = n_local // 2
+    chip, core = lane // 2, lax.rem(lane, 2)
+    sibling = chip * 2 + 1 - core
+    half = x_ref.shape[0] // HALVES
+    share = half // n_local
+    width = gpre.shape[3]
+    total = x_ref.shape[1]
+
+    def rows(h):
+        return slice(h * half, (h + 1) * half)
+
+    def remote(src, dst, send, recv, peer):
+        return pltpu.make_async_remote_copy(
+            src_ref=src, dst_ref=dst, send_sem=send, recv_sem=recv, device_id=(node, peer), device_id_type=MESH
+        )
+
+    def part_to(w, h, d):
+        peer = lax.rem(lane + d, n_local)
+        return remote(
+            rank_send.at[w, h, peer], rank_recv.at[w, h, lane], rank_ss.at[w, h, d], rank_rs.at[w, h, d], peer
+        )
+
+    def share_to(w, h, d):
+        peer = lax.rem(lane + d, n_local)
+        return remote(rank.at[w, h, lane], rank.at[w, h, lane], share_ss.at[w, h, d], share_rs.at[w, h, d], peer)
+
+    def to_sibling(h, y):
+        return remote(sib_send.at[h, y], sib_recv.at[h, y], sib_ss.at[h, y], sib_rs.at[h, y], sibling)
+
+    def pre_to(h, dy):
+        peer = lax.rem(chip + dy, chips) * 2 + core
+        return remote(pre_send.at[h, dy], pre_recv.at[h, dy], pre_ss.at[h, dy], pre_rs.at[h, dy], peer)
+
+    def gpre_to(h, dy):
+        peer = lax.rem(chip + dy, chips) * 2 + core
+        return remote(gpre.at[h, lane], gpre.at[h, lane], gp_ss.at[h, dy], gp_rs.at[h, dy], peer)
+
+    def forward(h, dy):
+        source = lax.rem(chip + chips - dy, chips) * 2 + core
+        return remote(gpre.at[h, source], gpre.at[h, source], fw_ss.at[h, dy], fw_rs.at[h, dy], sibling)
+
+    def each(count, act, first=0):
+        def body(i, carry):
+            act(i)
+            return carry
+
+        lax.fori_loop(first, count, body, 0)
+
+    my_columns = pl.ds(pl.multiple_of(lane * width, width), width)
+    loads = [
+        pltpu.make_async_copy(down_hbm, down, load_sem.at[0]),
+        pltpu.make_async_copy(up_hbm, up, load_sem.at[1]),
+        pltpu.make_async_copy(weight_hbm, weight, load_sem.at[2]),
+        pltpu.make_async_copy(grad_hbm.at[:, my_columns], hgrad, load_sem.at[3]),
+    ]
+    for load in loads:
+        load.start()
+
+    barrier = pltpu.get_barrier_semaphore()
+    each(
+        n_local,
+        lambda d: pl.semaphore_signal(
+            barrier, inc=1, device_id=(node, lax.rem(lane + d, n_local)), device_id_type=MESH
+        ),
+        1,
+    )
+    pl.semaphore_wait(barrier, n_local - 1)
+
+    def send_parts(w, h, part):
+        def columns(n):
+            here = pl.ds(pl.multiple_of(n * 256, 256), 256)
+            piece = part(here).astype(BF)
+            for t in range(n_local):
+                rank_send[w, h, t, :, here] = piece[t * share : (t + 1) * share]
+
+        each(rank.shape[4] // 256, columns)
+        each(n_local, lambda d: part_to(w, h, d).start(), 1)
+
+    def reduce_parts(w, h):
+        rank_recv[w, h, lane] = rank_send[w, h, lane]
+        each(n_local, lambda d: part_to(w, h, d).wait_recv(), 1)
+        summed = rank_recv[w, h, 0].astype(F32)
+        for t in range(1, n_local):
+            summed = summed + rank_recv[w, h, t].astype(F32)
+        rank[w, h, lane] = summed.astype(BF)
+        each(n_local, lambda d: share_to(w, h, d).start(), 1)
+
+    def whole_rank(w, h):
+        return rank[w, h].reshape(half, rank.shape[4])
+
+    def cross(h):
+        each(n_local, lambda d: share_to(0, h, d).wait_recv(), 1)
+
+        def columns(n):
+            here = pl.ds(pl.multiple_of(n * 256, 256), 256)
+            added = dot(whole_rank(0, h), up[:, here]) + bias_ref[:, here]
+            x = x_ref[rows(h), here].astype(F32)
+            result = (x * added + x).astype(BF)
+            term[rows(h), here] = added
+            inner[rows(h), here] = result
+            for i in range(2):
+                crossed_ref[n * 2 + i, rows(h), :] = result[:, i * 128 : (i + 1) * 128]
+
+        each(total // 256, columns)
+
+    def pre(h):
+        def part(t):
+            return dot(inner[rows(h), :], weight[:, pl.ds(pl.multiple_of(t * width, width), width)])
+
+        def other_core(y):
+            sib_send[h, y] = part(y * 2 + 1 - core).astype(BF)
+            to_sibling(h, y).start()
+
+        def my_core(i):
+            dy = lax.rem(i + 1, chips)
+            y = lax.rem(chip + dy, chips)
+            mine = part(y * 2 + core)
+            to_sibling(h, y).wait_recv()
+            mine = mine + sib_recv[h, y].astype(F32)
+
+            @pl.when(dy == 0)
+            def _():
+                pre_own[h] = mine
+
+            @pl.when(dy > 0)
+            def _():
+                pre_send[h, dy] = mine.astype(BF)
+                pre_to(h, dy).start()
+
+        each(chips, other_core)
+        each(chips, my_core)
+
+    def activate(h):
+        value = pre_own[h] + hbias_ref[:, my_columns]
+        for dy in range(1, chips):
+            pre_to(h, dy).wait_recv()
+            value = value + pre_recv[h, dy].astype(F32)
+        sig = jax.nn.sigmoid(value)
+        hidden_ref[rows(h), :] = (value * sig).astype(BF)
+        gpre[h, lane] = (hgrad[rows(h), :].astype(F32) * sig * (1.0 + value * (1.0 - sig))).astype(BF)
+        each(chips, lambda dy: gpre_to(h, dy).start(), 1)
+        forward(h, 0).start()
+
+    def pass_on(h):
+        def one(dy):
+            gpre_to(h, dy).wait_recv()
+            forward(h, dy).start()
+
+        each(chips, one, 1)
+
+    def back_chip(h, dy):
+        forward(h, dy).wait_recv()
+        y = lax.rem(chip + chips - dy, chips)
+        grads = jnp.concatenate([gpre[h, y * 2], gpre[h, y * 2 + 1]], 1)
+        wide = pl.ds(pl.multiple_of(y * 2 * width, 2 * width), 2 * width)
+
+        def columns(n):
+            here = pl.ds(pl.multiple_of(n * 256, 256), 256)
+            added = dot(grads, weight[here, wide], ((1,), (1,)))
+            if dy == 0:
+                gcross[rows(h), here] = added
+            else:
+                gcross[rows(h), here] += added
+
+        each(total // 256, columns)
+
+    def rank_grad(h):
+        inner[rows(h), :] = (gcross[rows(h), :] * x_ref[rows(h), :].astype(F32)).astype(BF)
+        send_parts(1, h, lambda here: dot(inner[rows(h), :], up[here, :], ((1,), (1,))))
+
+    def input_grad(h):
+        each(n_local, lambda d: share_to(1, h, d).wait_recv(), 1)
+
+        def columns(n):
+            here = pl.ds(pl.multiple_of(n * 256, 256), 256)
+            grads = gcross[rows(h), here]
+            result = grads * term[rows(h), here] + grads + dot(whole_rank(1, h), down[here, :], ((1,), (1,)))
+            result = result.astype(BF)
+            for i in range(2):
+                gx_ref[n * 2 + i, rows(h), :] = result[:, i * 128 : (i + 1) * 128]
+
+        each(total // 256, columns)
+
+    loads[0].wait()
+    for h in range(HALVES):
+        send_parts(0, h, lambda here: dot(x_ref[rows(h), :], down[:, here]))
+    for h in range(HALVES):
+        reduce_parts(0, h)
+    loads[1].wait()
+    for h in range(HALVES):
+        cross(h)
+        if h == 0:
+            loads[2].wait()
+        pre(h)
+    loads[3].wait()
+    for h in range(HALVES):
+        activate(h)
+    back_chip(0, 0)
+    pass_on(0)
+    for h in range(HALVES):
+        for dy in range(1, chips):
+            back_chip(h, dy)
+        if h + 1 < HALVES:
+            pass_on(h + 1)
+        rank_grad(h)
+        if h + 1 < HALVES:
+            back_chip(h + 1, 0)
+    for h in range(HALVES):
+        reduce_parts(1, h)
+    for h in range(HALVES):
+        input_grad(h)
+
+    for h in range(HALVES):
+        for w in range(2):
+            each(n_local, lambda d: part_to(w, h, d).wait_send(), 1)
+            each(n_local, lambda d: share_to(w, h, d).wait_send(), 1)
+        each(chips, lambda y: to_sibling(h, y).wait_send())
+        each(chips, lambda dy: pre_to(h, dy).wait_send(), 1)
+        each(chips, lambda dy: gpre_to(h, dy).wait_send(), 1)
+        each(chips, lambda dy: forward(h, dy).wait_send())
+
+
 SMEM = pl.BlockSpec(memory_space=pltpu.SMEM)
 VMEM = pl.BlockSpec(memory_space=pltpu.VMEM)
 SEM = pltpu.SemaphoreType.DMA
+ANY = pl.BlockSpec(memory_space=pl.ANY)
 
 
 def pool_and_send(pick, slot, picks, sizes, tables, n_node, n_local, cap, samples):
@@ -384,6 +615,56 @@
     )(pick, slot, picks, sizes, grads)
 
 
+def layers(x, bias, hidden_bias, hidden_grad, down, up, weight, features, n_local):
+    samples, total = x.shape
+    depth, hidden = down.shape[1], weight.shape[1]
+    half, width, chips = samples // HALVES, hidden // n_local, n_local // 2
+    parts = (2, HALVES, n_local, half // n_local, depth)
+    return pl.pallas_call(
+        functools.partial(layer_kernel, n_local),
+        out_shape=[
+            jax.ShapeDtypeStruct((features, samples, total // features), BF),
+            jax.ShapeDtypeStruct((samples, width), BF),
+            jax.ShapeDtypeStruct((features, samples, total // features), BF),
+        ],
+        in_specs=[VMEM, VMEM, VMEM, ANY, ANY, ANY, ANY],
+        out_specs=[VMEM, VMEM, VMEM],
+        scratch_shapes=[
+            pltpu.VMEM(down.shape, BF),
+            pltpu.VMEM(up.shape, BF),
+            pltpu.VMEM(weight.shape, BF),
+            pltpu.VMEM((samples, width), BF),
+            pltpu.VMEM(x.shape, F32),
+            pltpu.VMEM(x.shape, F32),
+            pltpu.VMEM(x.shape, BF),
+            pltpu.VMEM(parts, BF),
+            pltpu.VMEM(parts, BF),
+            pltpu.VMEM(parts, BF),
+            pltpu.VMEM((HALVES, chips, half, width), BF),
+            pltpu.VMEM((HALVES, chips, half, width), BF),
+            pltpu.VMEM((HALVES, chips, half, width), BF),
+            pltpu.VMEM((HALVES, chips, half, width), BF),
+            pltpu.VMEM((HALVES, half, width), F32),
+            pltpu.VMEM((HALVES, n_local, half, width), BF),
+            SEM((4,)),
+            SEM((2, HALVES, n_local)),
+            SEM((2, HALVES, n_local)),
+            SEM((2, HALVES, n_local)),
+            SEM((2, HALVES, n_local)),
+            SEM((HALVES, chips)),
+            SEM((HALVES, chips)),
+            SEM((HALVES, chips)),
+            SEM((HALVES, chips)),
+            SEM((HALVES, chips)),
+            SEM((HALVES, chips)),
+            SEM((HALVES, chips)),
+            SEM((HALVES, chips)),
+        ],
+        compiler_params=pltpu.CompilerParams(collective_id=2, has_side_effects=True, vmem_limit_bytes=56 << 20),
+        name="layers",
+    )(x, bias, hidden_bias, hidden_grad, down, up, weight)
+
+
 def on_device(
     owner_map,
     bag_sizes,
@@ -402,9 +683,7 @@
     capacity = node_count // lane_count + 1
     slot_total = lane_count * capacity
     samples = hidden_grad.shape[0]
-    emb_width = tables.shape[1]
     hidden_width = hidden_grad.shape[1]
-    share_width = hidden_width // lane_count
     picks = indices[0].T
     feat_ids = jnp.arange(owner_map.shape[0], dtype=jnp.int32)
     node_ids = jnp.arange(node_count, dtype=jnp.int32)
@@ -439,23 +718,17 @@
     down = cross_down.reshape(-1, cross_down.shape[2])
     up = cross_up.reshape(cross_up.shape[0], -1)
     weight = mlp_weight.reshape(-1, hidden_width)
-    partial_rank = dot(x_zero, down)
-    low_rank = lax.psum(partial_rank, "local").astype(BF)
-    cross_term = dot(low_rank, up) + cross_bias.reshape(1, -1)
-    x_float = x_zero.astype(F32)
-    crossed = (x_float * cross_term + x_float).astype(BF)
-    partial_pre = dot(crossed, weight)
-    share_start = my_lane * share_width
-    pre_act = lax.psum(partial_pre, "local") + mlp_bias
-    hidden = jax.nn.silu(lax.dynamic_slice_in_dim(pre_act, share_start, share_width, 1)).astype(BF)
-    sig_pre = jax.nn.sigmoid(pre_act)
-    grad_pre = (hidden_grad.astype(F32) * sig_pre * (1.0 + pre_act * (1.0 - sig_pre))).astype(BF)
-    grad_crossed = dot(grad_pre, weight, ((1,), (1,)))
-    grad_cross = (grad_crossed * x_float).astype(BF)
-    partial_grad_rank = dot(grad_cross, up, ((1,), (1,)))
-    grad_rank = lax.psum(partial_grad_rank.astype(BF), "local")
-    grad_input = grad_crossed * cross_term + grad_crossed + dot(grad_rank, down, ((1,), (1,)))
-    grad_input = grad_input.astype(BF).reshape(samples, node_count, emb_width).transpose(1, 0, 2)
+    crossed, hidden, grad_input = layers(
+        x_zero,
+        cross_bias.reshape(1, -1),
+        mlp_bias.reshape(1, -1),
+        hidden_grad,
+        down,
+        up,
+        weight,
+        node_count,
+        lane_count,
+    )
     table_grad = send_and_scatter(
         back_source,
         source_slot,
@@ -467,7 +740,6 @@
         lane_count,
         capacity,
     )
-    crossed = crossed.reshape(samples, node_count, emb_width).transpose(1, 0, 2)
     return (crossed, hidden, table_grad)
 
 

time: 377 us -> 208 us (0.55)
  waiting for transfers between devices: 126 us -> 0 us
  Pallas kernels: 120 us -> 194 us
  blocking collectives: 49.3 us -> 0 us
  matrix products: 36.6 us -> 0 us
  between operations: 14.2 us -> 0.73 us
  local copies, waits for them, and re-layouts: 21.1 us -> 8.97 us
  other arithmetic: 8.21 us -> 3.4 us
    psum x2 -> x0, waiting for transfers between devices: 126 us -> none  [the longest x1 71.3 us: on_device(): pre_act = lax.psum(partial_pre, 'local') + mlp_bias]
    pallas_call x0 -> x1, Pallas kernels: none -> 77.3 us  [layers(): pl.pallas_call(functools.partial(layer_kernel, n_local), out_shape=[jax.S...]
    psum x1 -> x0, blocking collectives: 49.3 us -> none  [on_device(): low_rank = lax.psum(partial_rank, 'local').astype(BF)]
    dot_general x6 -> x0, matrix products: 36.6 us -> none  [dot(): lax.dot_general(a, b, (contract, ((), ())), preferred_element_type=F32)]
    convert_element_type x1 -> x0, local copies, waits for them, and re-layouts: 3.93 us -> none  [on_device(): grad_input.astype(BF).reshape(samples, node_count, emb_width)]
    reshape x1 -> x0, local copies, waits for them, and re-layouts: 3.92 us -> none  [on_device(): grad_input.astype(BF).reshape(samples, node_count, emb_width)]
    unnamed x29 -> x22, local copies, waits for them, and re-layouts: 9.76 us -> 8.97 us
  transfers between devices with their start and end apart: 2 -> 0, of which waited for: 2 -> 0; matrix products, arithmetic and copies ran while one was open for 2% -> 0% of each run, Pallas kernels for 0% -> 0%
where the time goes in v2:
time: 208 us; the launch traced here: 207 us
  Pallas kernels  194 us (93%)
  local copies, waits for them, and re-layouts  8.97 us (4%)
  other arithmetic  3.4 us (2%)
    pallas_call x1, Pallas kernels, layers(): pl.pallas_call(functools.partial(layer_kernel, n_local), out_shape=[jax.S...  77.3 us
    pallas_call x1, Pallas kernels, pool_and_send(): pl.pallas_call(functools.partial(pool_kernel, n_node, n_local), out_shape...  62.3 us
    pallas_call x1, Pallas kernels, send_and_scatter(): pl.pallas_call(functools.partial(scatter_kernel, n_node, n_local), out_sh...  54.5 us
    unnamed x22, local copies, waits for them, and re-layouts  8.97 us

profile of v2, /device:TPU:1, one launch (start us, length us, event | category | flops | bytes accessed | tf_op | source)
XLA Modules:
  0.0 207.2 jit_solution(9526406465844965925)
XLA Ops:
  0.6 0.8 select_reduce_fusion.2
  1.5 0.2 convert_reduce_fusion.1
  1.7 0.0 copy-start.8
  1.7 0.1 select_reduce_fusion.1.pick_ref
  1.8 0.7 and_select_fusion.1
  2.5 0.7 and_select_fusion
  3.3 0.2 convert_reduce_fusion
  3.5 0.6 select_reduce_fusion.pick_ref
  4.1 0.9 copy-done.1
  5.0 1.0 copy-done.2
  6.1 0.8 copy-done.3
  6.8 62.3 %pool_and_send.1.x_ref = bf16[512,2048]{1,0:T(8,128)(2,1)S(1)} custom-call(s32[24]{0:T(128)S(1)} %select_reduce_fusion.1.pick_ref, s32[16]{0:T(128)S(1)} %multiply_add_fusion.slot_ref, s32[8,8192]{1,0:T(8,128)S(1)} %bitcast.12, s32[1,8192]{1,0:T(1,128)S(1)} %copy-done.3, bf16[2048,128]{1,0:T(8,128)(2,1)S(1)} %copy-done.2), custom_call_target="tpu_custom_call" | custom-call | tf_op jit(solution)/shard_map/pool_and_send/pallas_call | solution.py:564
  69.1 0.0 copy-start
  69.1 1.3 copy-done
  70.4 1.9 copy.15
  72.3 77.3 %layers.1 = (bf16[16,512,128]{2,1,0:T(8,128)(2,1)}, bf16[512,256]{1,0:T(8,128)(2,1)}, bf16[16,512,128]{2,1,0:T(8,128)(2,1)}) custom-call(bf16[512,2048]{1,0:T(8,128)(2,1)} %copy-done, f32[1,2048]{1,0:T(1,128)} %bitcast.17, f32[1,2048]{1,0:T(1,128)} %bitcast.18, bf16[512,2048]{1,0:T(8,128)(2,1)} %grad_hbm.1, bf16[2048,512]{1,0:T(8,128)(2,1)} %bitcast.15, ...), custom_call_target="tpu_custom_call" | custom-call | tf_op jit(solution)/shard_map/layers/pallas_call | solution.py:623
  149.6 54.5 %send_and_scatter.1 = f32[2048,128]{1,0:T(8,128)} custom-call(s32[24]{0:T(128)} %select_reduce_fusion.pick_ref, s32[16]{0:T(128)} %copy-done.8, s32[8,8192]{1,0:T(8,128)} %bitcast.11, s32[1,8192]{1,0:T(1,128)} %size_ref.3, bf16[16,512,128]{2,1,0:T(8,128)(2,1)} %get-tuple-element.8.grad_ref), custom_call_target="tpu_custom_call" | custom-call | tf_op jit(solution)/shard_map/send_and_scatter/pallas_call | solution.py:592
  204.2 0.0 copy-done.6
  204.2 0.0 copy-start.7
  204.2 0.0 copy-start.4
  204.2 1.3 copy.19
  205.5 0.7 copy.20
  206.2 0.0 copy-done.4
  206.3 1.0 copy.21
  (12 shorter events, 0.1 us)
Async XLA Ops:
  1.7 70.6 %copy-start.8 = (s32[16]{0:T(128)}, s32[16]{0:T(128)S(1)}, u32[]{:S(2)}) copy-start(s32[16]{0:T(128)S(1)} %multiply_add_fusion.1.slot_ref) | copy-start | bytes 196
  4.1 0.9 copy-start.1
  5.0 1.0 copy-start.2
  6.1 0.8 copy-start.3
  6.8 63.6 %copy-start.5 = (bf16[512,16,128]{2,1,0:T(8,128)(2,1)S(1)}, bf16[512,16,128]{2,1,0:T(8,128)(2,1)}, u32[]{:S(2)}) copy-start(bf16[512,16,128]{2,1,0:T(8,128)(2,1)} %param.15) | copy-start | bytes 6291460
  69.1 1.3 copy-start
  149.6 54.5 %copy-start.6 = (bf16[16,512,128]{2,1,0:T(8,128)(2,1)S(1)}, bf16[16,512,128]{2,1,0:T(8,128)(2,1)}, u32[]{:S(2)}) copy-start(bf16[16,512,128]{2,1,0:T(8,128)(2,1)} %get-tuple-element.14) | copy-start | bytes 6291460
  204.2 1.3 copy-start.7
  204.2 2.1 copy-start.4

commit v3 on v0

v3 whole, which is shorter than its diff:
```python
import functools
import types

import jax
import jax.numpy as jnp
from jax import lax
from jax.experimental import pallas as pl
from jax.experimental.pallas import tpu as pltpu
from jax.sharding import PartitionSpec as P

BF = jnp.bfloat16
F32 = jnp.float32
MESH = pl.DeviceIdType.MESH
PIECES = 4
HALVES = 2
CHUNK = 16
VMEM_LIMIT = 62 << 20
BAG_GROUP = 32
LOW = 256


def dot(a, b, contract=((1,), (0,))):
    return lax.dot_general(a, b, (contract, ((), ())), preferred_element_type=F32)


def greet(n_node, n_local, node, lane):
    barrier = pltpu.get_barrier_semaphore()

    def by_node(k, carry):
        peer = lax.rem(node + k, n_node)
        pl.semaphore_signal(barrier, inc=1, device_id=(peer, lane), device_id_type=MESH)
        return carry

    def by_lane(d, carry):
        peer = lax.rem(lane + d, n_local)
        pl.semaphore_signal(barrier, inc=1, device_id=(node, peer), device_id_type=MESH)
        return carry

    lax.fori_loop(1, n_node, by_node, 0)
    lax.fori_loop(1, n_local, by_lane, 0)
    pl.semaphore_wait(barrier, n_node + n_local - 2)


def flatten_picks(idx_ref, size_ref, iota_ref, key_ref, low_ref):
    iota_ref[...] = lax.broadcasted_iota(jnp.int32, iota_ref.shape, 0).astype(F32).astype(BF)
    lanes = lax.broadcasted_iota(jnp.int32, (1, 128), 1)
    depth = lax.broadcasted_iota(jnp.int32, (8, 128), 0)

    def eight_groups(b, carry):
        rows = [[], []]
        for half in range(2):
            off = pl.multiple_of(b * 256 + half * 128, 128)
            picks = jnp.where(depth < size_ref[:, pl.ds(off, 128)], idx_ref[:, pl.ds(off, 128)], -1)
            turned = [picks] + [pltpu.roll(picks, 32 * d, 1) for d in (1, 2, 3)]
            for group in range(4):
                for h in range(2):
                    row = turned[(3 - group) % 4][4 * h + 3 : 4 * h + 4]
                    for q in (2, 1, 0):
                        source = turned[(q - group) % 4][4 * h + q : 4 * h + q + 1]
                        row = jnp.where(lanes < 32 * (q + 1), source, row)
                    rows[h].append(row)
        here = pl.ds(pl.multiple_of(b * 8, 8), 8)
        for h in range(2):
            picks = jnp.concatenate(rows[h], 0)
            key_ref[here, h * 128 : (h + 1) * 128] = ((picks >> 8) * 32 + (lanes & 31)).astype(F32)
            low_ref[here, h * 128 : (h + 1) * 128] = (picks & 255).astype(F32)
        return carry

    lax.fori_loop(0, idx_ref.shape[1] // 256, eight_groups, 0)


def count_group(key_ref, low_ref, iota_ref, group):
    iota = iota_ref[...]
    one, zero = jnp.ones((), BF), jnp.zeros((), BF)
    hot = []
    for ref in (key_ref, low_ref):
        row = jnp.broadcast_to(ref[pl.ds(group, 1), :], (16, LOW)).astype(BF)
        hot.append(jnp.where(jnp.concatenate([row] * 16, 0) == iota, one, zero))
    return dot(hot[0], hot[1], ((1,), (1,))).astype(BF)


def put_counts(count_ref, where, row, counts):
    for h in range(8):
        count_ref[where, pl.ds(row, BAG_GROUP), h * LOW : (h + 1) * LOW] = counts[h * 32 : (h + 1) * 32]


def step_kernel(names, n_node, n_local, *refs):
    r = types.SimpleNamespace(**dict(zip(names, refs)))
    node, lane = lax.axis_index("node"), lax.axis_index("local")
    chips = n_local // 2
    chip, core = lane // 2, lax.rem(lane, 2)
    sibling = chip * 2 + 1 - core
    cap, small = r.packed.shape[2], r.packed.shape[3]
    samples, total = r.x.shape
    half = samples // HALVES
    share = half // n_local
    width = r.gpre.shape[3]
    per_node = samples // BAG_GROUP
    chunks = n_node * small // (CHUNK * BAG_GROUP)
    arrived = [getattr(r, f"arrived{p}") for p in range(PIECES)]
    landed = [getattr(r, f"landed{p}") for p in range(PIECES)]
    returned = [getattr(r, f"returned{p}") for p in range(PIECES)]

    def rows(h):
        return slice(h * half, (h + 1) * half)

    def each(count, act, first=0):
        def body(i, carry):
            act(i)
            return carry

        lax.fori_loop(first, count, body, 0)

    def remote(src, dst, sems, at, peer):
        send, recv = sems
        return pltpu.make_async_remote_copy(
            src_ref=src, dst_ref=dst, send_sem=send.at[at], recv_sem=recv.at[at], device_id=peer, device_id_type=MESH
        )

    def node_peer(k):
        return lax.rem(node + k, n_node), lane

    def lane_peer(d):
        return node, lax.rem(lane + d, n_local)

    def chip_peer(dy):
        return node, lax.rem(chip + dy, chips) * 2 + core

    def out_node(p, k):
        return remote(r.pooled.at[p, k], arrived[p].at[node], (r.on_s, r.on_r), (p, k), node_peer(k))

    def out_lane(p, d):
        here = pl.ds(lane * cap, cap)
        return remote(r.packed.at[p, d], landed[p].at[here], (r.ol_s, r.ol_r), (p, d), lane_peer(d))

    def back_lane(p, d):
        here = pl.ds(lane * cap, cap)
        return remote(r.packed.at[p, d], returned[p].at[here], (r.bl_s, r.bl_r), (p, d), lane_peer(d))

    def back_node(p, k):
        return remote(r.pooled.at[p, k], r.home.at[p, node], (r.bn_s, r.bn_r), (p, k), node_peer(k))

    def part_to(w, h, d):
        peer = lane_peer(d)
        return remote(r.rank_send.at[w, h, peer[1]], r.rank_recv.at[w, h, lane], (r.rk_s, r.rk_r), (w, h, d), peer)

    def share_to(w, h, d):
        return remote(r.rank.at[w, h, lane], r.rank.at[w, h, lane], (r.sh_s, r.sh_r), (w, h, d), lane_peer(d))

    def to_sibling(h, y):
        return remote(r.sib_send.at[h, y], r.sib_recv.at[h, y], (r.sb_s, r.sb_r), (h, y), (node, sibling))

    def pre_to(h, dy):
        return remote(r.pre_send.at[h, dy], r.pre_recv.at[h, dy], (r.pr_s, r.pr_r), (h, dy), chip_peer(dy))

    def gpre_to(h, dy):
        return remote(r.gpre.at[h, lane], r.gpre.at[h, lane], (r.gp_s, r.gp_r), (h, dy), chip_peer(dy))

    def forward(h, dy):
        source = lax.rem(chip + chips - dy, chips) * 2 + core
        return remote(r.gpre.at[h, source], r.gpre.at[h, source], (r.fw_s, r.fw_r), (h, dy), (node, sibling))

    def save(t):
        buffer = lax.rem(t, 2)
        return pltpu.make_async_copy(r.counts.at[buffer], r.kept.at[t], r.save_sem.at[buffer])

    def fetch(t):
        buffer = lax.rem(t, 2)
        return pltpu.make_async_copy(r.kept.at[t], r.counts.at[buffer], r.fetch_sem.at[buffer])

    def pool_piece(p):
        def one_chunk(c):
            t = p * chunks + c

            @pl.when(t >= 2)
            def _():
                save(t - 2).wait()

            buffer = lax.rem(t, 2)
            for i in range(CHUNK):
                source = lax.rem(node + c * 4 + i // 4, n_node)
                group = source * per_node + p * 4 + i % 4
                put_counts(r.counts, buffer, i * BAG_GROUP, count_group(r.key, r.low, r.iota, group))
            save(t).start()
            sums = dot(r.counts[buffer], r.table[...]).astype(BF)
            for i in range(4):
                r.pooled[p, c * 4 + i] = sums[i * small : (i + 1) * small]
            for piece in range(PIECES):

                @pl.when(p == piece)
                def _():
                    each(c * 4 + 4, lambda k: out_node(piece, k).start(), jnp.maximum(c * 4, 1))

        each(chunks, one_chunk)

    def pack_piece(p):
        each(n_node, lambda k: out_node(p, k).wait_recv(), 1)
        arrived[p][node] = r.pooled[p, 0]

        def send(d):
            target = lax.rem(lane + d, n_local)
            for c in range(cap):
                r.packed[p, d, c] = arrived[p][r.pick[target * cap + c]]
            out_lane(p, d).start()

        each(n_local, send, 1)
        for c in range(cap):
            landed[p][lane * cap + c] = arrived[p][r.pick[lane * cap + c]]

    def unpack_piece(p):
        each(n_local, lambda d: out_lane(p, d).wait_recv(), 1)
        for q in range(n_node):
            r.x[p * small : (p + 1) * small, q * 128 : (q + 1) * 128] = landed[p][r.slot[q]]

    def send_parts(w, h, part):
        def columns(n):
            here = pl.ds(pl.multiple_of(n * 256, 256), 256)
            piece = part(here).astype(BF)
            for t in range(n_local):
                r.rank_send[w, h, t, :, here] = piece[t * share : (t + 1) * share]

        each(r.rank.shape[4] // 256, columns)
        each(n_local, lambda d: part_to(w, h, d).start(), 1)

    def reduce_parts(w, h):
        r.rank_recv[w, h, lane] = r.rank_send[w, h, lane]
        each(n_local, lambda d: part_to(w, h, d).wait_recv(), 1)
        summed = r.rank_recv[w, h, 0].astype(F32)
        for t in range(1, n_local):
            summed = summed + r.rank_recv[w, h, t].astype(F32)
        r.rank[w, h, lane] = summed.astype(BF)
        each(n_local, lambda d: share_to(w, h, d).start(), 1)

    def whole_rank(w, h):
        return r.rank[w, h].reshape(half, r.rank.shape[4])

    def side_by_side(ref, h):
        return jnp.concatenate([ref[q, rows(h), :] for q in range(n_node)], 1)

    def low_parts(h):
        send_parts(0, h, lambda here: dot(r.x[rows(h), :], r.down[:, here]))

    def cross(h):
        each(n_local, lambda d: share_to(0, h, d).wait_recv(), 1)

        def columns(n):
            here = pl.ds(pl.multiple_of(n * 512, 512), 512)
            added = dot(whole_rank(0, h), r.up[:, here]) + r.bias[:, here]
            x = r.x[rows(h), here].astype(F32)
            result = (x * added + x).astype(BF)
            r.term[rows(h), here] = added
            for i in range(4):
                r.crossed[n * 4 + i, rows(h), :] = result[:, i * 128 : (i + 1) * 128]

        each(total // 512, columns)

    def pre(h):
        def part(t):
            return dot(side_by_side(r.crossed, h), r.weight[:, pl.ds(pl.multiple_of(t * width, width), width)])

        def other_core(y):
            r.sib_send[h, y] = part(y * 2 + 1 - core).astype(BF)
            to_sibling(h, y).start()

        def my_core(i):
            dy = lax.rem(i + 1, chips)
            y = lax.rem(chip + dy, chips)
            mine = part(y * 2 + core)
            to_sibling(h, y).wait_recv()
            mine = mine + r.sib_recv[h, y].astype(F32)

            @pl.when(dy == 0)
            def _():
                r.pre_own[h] = mine

            @pl.when(dy > 0)
            def _():
                r.pre_send[h, dy] = mine.astype(BF)
                pre_to(h, dy).start()

        each(chips, other_core)
        each(chips, my_core)

    def activate(h):
        value = r.pre_own[h] + r.hbias[:, pl.ds(pl.multiple_of(lane * width, width), width)]
        for dy in range(1, chips):
            pre_to(h, dy).wait_recv()
            value = value + r.pre_recv[h, dy].astype(F32)
        sig = jax.nn.sigmoid(value)
        r.hidden[rows(h), :] = (value * sig).astype(BF)
        r.gpre[h, lane] = (r.hgrad[rows(h), :].astype(F32) * sig * (1.0 + value * (1.0 - sig))).astype(BF)
        each(chips, lambda dy: gpre_to(h, dy).start(), 1)
        forward(h, 0).start()

    def pass_on(h):
        def one(dy):
            gpre_to(h, dy).wait_recv()
            forward(h, dy).start()

        each(chips, one, 1)

    def back_chips(h, steps):
        sides = []
        for dy in steps:
            forward(h, dy).wait_recv()
            y = lax.rem(chip + chips - dy, chips)
            wide = pl.ds(pl.multiple_of(y * 2 * width, 2 * width), 2 * width)
            sides.append((y, wide))

        def columns(n):
            here = pl.ds(pl.multiple_of(n * 512, 512), 512)
            added = None
            for y, wide in sides:
                grads = jnp.concatenate([r.gpre[h, y * 2], r.gpre[h, y * 2 + 1]], 1)
                term = dot(grads, r.weight[here, wide], ((1,), (1,)))
                added = term if added is None else added + term
            if 0 in steps:
                r.gcross[rows(h), here] = added
            else:
                r.gcross[rows(h), here] += added

        each(total // 512, columns)

    def rank_grad(h):
        for q in range(n_node):
            here = slice(q * 128, (q + 1) * 128)
            r.gx[q, rows(h), :] = (r.gcross[rows(h), here] * r.x[rows(h), here].astype(F32)).astype(BF)
        send_parts(1, h, lambda here: dot(side_by_side(r.gx, h), r.up[here, :], ((1,), (1,))))

    def input_grad(h):
        each(n_local, lambda d: share_to(1, h, d).wait_recv(), 1)

        def columns(n):
            here = pl.ds(pl.multiple_of(n * 512, 512), 512)
            grads = r.gcross[rows(h), here]
            result = grads * r.term[rows(h), here] + grads + dot(whole_rank(1, h), r.down[here, :], ((1,), (1,)))
            result = result.astype(BF)
            for i in range(4):
                r.gx[n * 4 + i, rows(h), :] = result[:, i * 128 : (i + 1) * 128]

        each(total // 512, columns)

    def pack_back(p):
        here = slice(p * small, (p + 1) * small)
        each(n_local, lambda d: out_lane(p, d).wait_send(), 1)

        def send(d):
            target = lax.rem(lane + d, n_local)
            for c in range(cap):
                r.packed[p, d, c] = r.gx[r.back_pick[target * cap + c], here]
            back_lane(p, d).start()

        each(n_local, send, 1)
        for c in range(cap):
            returned[p][lane * cap + c] = r.gx[r.back_pick[lane * cap + c], here]

    def route_piece(p):
        each(n_node, lambda k: out_node(p, k).wait_send(), 1)
        each(n_local, lambda d: back_lane(p, d).wait_recv(), 1)

        def send(k):
            r.pooled[p, k] = returned[p][r.back_slot[lax.rem(node + k, n_node)]]
            back_node(p, k).start()

        each(n_node, send, 1)
        r.home[p, node] = returned[p][r.back_slot[node]]

    def add_piece(p):
        each(n_node, lambda k: back_node(p, k).wait_recv(), 1)

        def one_chunk(c):
            t = p * chunks + c
            buffer = lax.rem(t, 2)
            for i in range(4):
                r.home_t[:, i * small : (i + 1) * small] = r.home[p, lax.rem(node + c * 4 + i, n_node)].T
            fetch(t).wait()
            for n in range(r.sums.shape[1] // 512):
                here = slice(n * 512, (n + 1) * 512)
                r.sums[:, here] += dot(r.home_t[...], r.counts[buffer, :, here])

            @pl.when(t + 2 < PIECES * chunks)
            def _():
                fetch(t + 2).start()

        each(chunks, one_chunk)

    my_columns = pl.ds(pl.multiple_of(lane * width, width), width)
    loads = [
        pltpu.make_async_copy(r.down_hbm, r.down, r.load_sem.at[0]),
        pltpu.make_async_copy(r.up_hbm, r.up, r.load_sem.at[1]),
        pltpu.make_async_copy(r.weight_hbm, r.weight, r.load_sem.at[2]),
        pltpu.make_async_copy(r.grad_hbm.at[:, my_columns], r.hgrad, r.load_sem.at[3]),
    ]
    for load in loads:
        load.start()
    greet(n_node, n_local, node, lane)
    flatten_picks(r.idx, r.size, r.iota, r.key, r.low)
    r.sums[...] = jnp.zeros_like(r.sums)

    def turn(p):
        pool_piece(p)
        for piece in range(PIECES - 1):

            @pl.when(p == piece + 1)
            def _():
                pack_piece(piece)

    each(PIECES, turn)
    pack_piece(PIECES - 1)
    for t in range(2):
        save(PIECES * chunks - 2 + t).wait()
    for t in range(2):
        fetch(t).start()
    for load in loads:
        load.wait()
    per_half = PIECES // HALVES
    for h in range(HALVES):
        for p in range(h * per_half, (h + 1) * per_half):
            unpack_piece(p)
        low_parts(h)
    for h in range(HALVES):
        reduce_parts(0, h)
    for h in range(HALVES):
        cross(h)
        pre(h)
    for h in range(HALVES):
        activate(h)
    back_chips(0, [0])
    pass_on(0)
    back_chips(0, [1, 2, 3])
    pass_on(1)
    rank_grad(0)
    back_chips(1, [0, 1, 2, 3])
    reduce_parts(1, 0)
    rank_grad(1)
    input_grad(0)
    pack_back(0)
    pack_back(1)
    reduce_parts(1, 1)
    input_grad(1)
    pack_back(2)
    pack_back(3)
    route_piece(0)
    route_piece(1)
    add_piece(0)
    route_piece(2)
    add_piece(1)
    route_piece(3)
    add_piece(2)
    add_piece(3)
    for n in range(r.sums.shape[1] // 128):
        r.table_grad[n * 128 : (n + 1) * 128, :] = r.sums[:, n * 128 : (n + 1) * 128].T

    for p in range(PIECES):
        each(n_node, lambda k: back_node(p, k).wait_send(), 1)
        each(n_local, lambda d: back_lane(p, d).wait_send(), 1)
    for h in range(HALVES):
        for w in range(2):
            each(n_local, lambda d: part_to(w, h, d).wait_send(), 1)
            each(n_local, lambda d: share_to(w, h, d).wait_send(), 1)
        each(chips, lambda y: to_sibling(h, y).wait_send())
        each(chips, lambda dy: pre_to(h, dy).wait_send(), 1)
        each(chips, lambda dy: gpre_to(h, dy).wait_send(), 1)
        each(chips, lambda dy: forward(h, dy).wait_send())


SMEM = pl.BlockSpec(memory_space=pltpu.SMEM)
VMEM = pl.BlockSpec(memory_space=pltpu.VMEM)
ANY = pl.BlockSpec(memory_space=pl.ANY)
SEM = pltpu.SemaphoreType.DMA


def train_step(operands, features, samples, n_node, n_local, cap):
    depth, hidden = operands["down_hbm"].shape[1], operands["weight_hbm"].shape[1]
    total = operands["down_hbm"].shape[0]
    table_rows, emb = operands["table"].shape
    groups = operands["idx"].shape[1] // BAG_GROUP
    small, half, width, chips = samples // PIECES, samples // HALVES, hidden // n_local, n_local // 2
    kept = (groups // CHUNK, CHUNK * BAG_GROUP, table_rows)
    outs = {
        "crossed": (jax.ShapeDtypeStruct((features, samples, emb), BF), VMEM),
        "hidden": (jax.ShapeDtypeStruct((samples, width), BF), VMEM),
        "table_grad": (jax.ShapeDtypeStruct((table_rows, emb), F32), VMEM),
        "kept": (jax.ShapeDtypeStruct(kept, BF), ANY),
    }
    parts = pltpu.VMEM((2, HALVES, n_local, half // n_local, depth), BF)
    quarter = pltpu.VMEM((HALVES, chips, half, width), BF)
    scratch = {
        "iota": pltpu.VMEM((LOW, LOW), BF),
        "key": pltpu.VMEM((groups, LOW), F32),
        "low": pltpu.VMEM((groups, LOW), F32),
        "counts": pltpu.VMEM((2, *kept[1:]), BF),
        "pooled": pltpu.VMEM((PIECES, n_node, small, emb), BF),
        "packed": pltpu.VMEM((PIECES, n_local, cap, small, emb), BF),
        "home": pltpu.VMEM((PIECES, n_node, small, emb), BF),
        "home_t": pltpu.VMEM((emb, 4 * small), BF),
        "sums": pltpu.VMEM((emb, table_rows), F32),
        "x": pltpu.VMEM((samples, total), BF),
        "down": pltpu.VMEM((total, depth), BF),
        "up": pltpu.VMEM((depth, total), BF),
        "weight": pltpu.VMEM((total, hidden), BF),
        "hgrad": pltpu.VMEM((samples, width), BF),
        "term": pltpu.VMEM((samples, total), F32),
        "gcross": pltpu.VMEM((samples, total), F32),
        "gx": pltpu.VMEM((features, samples, emb), BF),
        "rank_send": parts,
        "rank_recv": parts,
        "rank": parts,
        "sib_send": quarter,
        "sib_recv": quarter,
        "pre_send": quarter,
        "pre_recv": quarter,
        "pre_own": pltpu.VMEM((HALVES, half, width), F32),
        "gpre": pltpu.VMEM((HALVES, n_local, half, width), BF),
        "load_sem": SEM((4,)),
        "save_sem": SEM((2,)),
        "fetch_sem": SEM((2,)),
    }
    for p in range(PIECES):
        scratch[f"arrived{p}"] = pltpu.VMEM((n_node, small, emb), BF)
        scratch[f"landed{p}"] = pltpu.VMEM((n_local * cap, small, emb), BF)
        scratch[f"returned{p}"] = pltpu.VMEM((n_local * cap, small, emb), BF)
    for names, shape in (
        (("on", "bn"), (PIECES, n_node)),
        (("ol", "bl"), (PIECES, n_local)),
        (("rk", "sh"), (2, HALVES, n_local)),
        (("sb", "pr", "gp", "fw"), (HALVES, chips)),
    ):
        for name in names:
            scratch[name + "_s"] = SEM(shape)
            scratch[name + "_r"] = SEM(shape)
    places = {"pick": SMEM, "slot": SMEM, "back_pick": SMEM, "back_slot": SMEM}
    specs = [places.get(name, ANY if name.endswith("_hbm") else VMEM) for name in operands]
    names = [*operands, *outs, *scratch]
    return pl.pallas_call(
        functools.partial(step_kernel, names, n_node, n_local),
        out_shape=[shape for shape, _ in outs.values()],
        in_specs=specs,
        out_specs=[spec for _, spec in outs.values()],
        scratch_shapes=list(scratch.values()),
        compiler_params=pltpu.CompilerParams(collective_id=0, has_side_effects=True, vmem_limit_bytes=VMEM_LIMIT),
        name="train_step",
    )(*operands.values())


def on_device(
    owner_map,
    bag_sizes,
    indices,
    tables,
    cross_down,
    cross_up,
    cross_bias,
    mlp_weight,
    mlp_bias,
    hidden_grad,
):
    node_count = lax.axis_size("node")
    lane_count = lax.axis_size("local")
    my_lane = lax.axis_index("local")
    capacity = node_count // lane_count + 1
    slot_total = lane_count * capacity
    samples = hidden_grad.shape[0]
    hidden_width = hidden_grad.shape[1]
    feat_ids = jnp.arange(owner_map.shape[0], dtype=jnp.int32)
    node_ids = jnp.arange(node_count, dtype=jnp.int32)
    source_dev = node_ids * lane_count + my_lane
    source_feat = jnp.sum(
        jnp.where(owner_map[None, :] == source_dev[:, None], feat_ids[None, :], 0), axis=1
    )
    source_group = source_feat // node_count
    same_group = source_group[:, None] == source_group[None, :]
    earlier = node_ids[None, :] < node_ids[:, None]
    source_slot = source_group * capacity + jnp.sum(
        (same_group & earlier).astype(jnp.int32), axis=1
    )
    group_owners = lax.dynamic_slice_in_dim(owner_map, my_lane * node_count, node_count)
    owner_lane = group_owners % lane_count
    owner_node = group_owners // lane_count
    ahead_same = (owner_lane[:, None] == owner_lane[None, :]) & (
        owner_node[None, :] < owner_node[:, None]
    )
    owner_slot = owner_lane * capacity + jnp.sum(ahead_same.astype(jnp.int32), axis=1)
    slot_ids = jnp.arange(slot_total, dtype=jnp.int32)
    pick_source = jnp.sum(
        jnp.where(source_slot[None, :] == slot_ids[:, None], node_ids[None, :], 0), axis=1
    )
    back_source = jnp.sum(
        jnp.where(owner_slot[None, :] == slot_ids[:, None], node_ids[None, :], 0), axis=1
    )

    operands = {
        "pick": pick_source,
        "slot": owner_slot,
        "back_pick": back_source,
        "back_slot": source_slot,
        "idx": indices[0].T,
        "size": bag_sizes,
        "table": tables,
        "bias": cross_bias.reshape(1, -1),
        "hbias": mlp_bias.reshape(1, -1),
        "grad_hbm": hidden_grad,
        "down_hbm": cross_down.reshape(-1, cross_down.shape[2]),
        "up_hbm": cross_up.reshape(cross_up.shape[0], -1),
        "weight_hbm": mlp_weight.reshape(-1, hidden_width),
    }
    crossed, hidden, table_grad, _ = train_step(operands, node_count, samples, node_count, lane_count, capacity)
    return (crossed, hidden, table_grad)


def solution(mesh):
    return jax.shard_map(
        on_device,
        mesh=mesh,
        in_specs=(
            P(),
            P(("node", "local"), None),
            P(("node", "local"), None, None),
            P(("node", "local"), None),
            P("local", None, None),
            P(None, "local", None),
            P("local", None),
            P("local", None, None),
            P(),
            P("node", None),
        ),
        out_specs=(P("local", "node", None), P("node", "local"), P(("node", "local"), None)),
        check_vma=False,
    )
```

time: 747 us -> 191 us (0.26)
  matrix products: 322 us -> 0 us
  waiting for transfers between devices: 252 us -> 0 us
  Pallas kernels: 0 us -> 178 us
  blocking collectives: 50.5 us -> 0 us
  local copies, waits for them, and re-layouts: 48.5 us -> 8.35 us
  starting transfers between devices: 30.5 us -> 0 us
  other arithmetic: 21.1 us -> 3.32 us
  between operations: 14.2 us -> 0.69 us
    dot_general x38 -> x0, matrix products: 322 us -> none  [the longest x16 145 us: add_block(): lax.dot_general(matrix, grad_rows, (((0,), (0,)), ((), ())), preferred_el...]
    pallas_call x0 -> x1, Pallas kernels: none -> 178 us  [train_step(): pl.pallas_call(functools.partial(step_kernel, names, n_node, n_local), ou...]
    psum x2 -> x0, waiting for transfers between devices: 130 us -> none  [the longest x1 68.9 us: on_device(): pre_act = lax.psum(partial_pre, 'local') + mlp_bias]
    all_to_all x4 -> x0, waiting for transfers between devices: 123 us -> none  [the longest x1 37.7 us: on_device(): lax.all_to_all(back_packed.reshape(lane_count, capacity, samples, emb_wid...]
    psum x1 -> x0, blocking collectives: 50.5 us -> none  [on_device(): low_rank = lax.psum(partial_rank, 'local').astype(jnp.bfloat16)]
    all_to_all x4 -> x0, starting transfers between devices: 30.3 us -> none  [the longest x1 8.61 us: on_device(): lax.all_to_all(outgoing, 'node', split_axis=0, concat_axis=0, tiled=True)]
    squeeze x32 -> x0, local copies, waits for them, and re-layouts: 23 us -> none  [on_device(): lax.map(pool_block, (pick_blocks, count_blocks))]
    gather x4 -> x0, local copies, waits for them, and re-layouts: 16.8 us -> none  [the longest x1 4.36 us: on_device(): jnp.take(grad_input, back_source, axis=0)]
  transfers between devices with their start and end apart: 6 -> 0, of which waited for: 6 -> 0; matrix products, arithmetic and copies ran while one was open for 1% -> 0% of each run, Pallas kernels for 0% -> 0%
where the time goes in v3:
time: 191 us; the launch traced here: 190 us
  Pallas kernels  178 us (93%)
  local copies, waits for them, and re-layouts  8.35 us (4%)
  other arithmetic  3.32 us (2%)
    pallas_call x1, Pallas kernels, train_step(): pl.pallas_call(functools.partial(step_kernel, names, n_node, n_local), ou...  178 us
    unnamed x12, local copies, waits for them, and re-layouts  8.35 us

profile of v3, /device:TPU:1, one launch (start us, length us, event | category | flops | bytes accessed | tf_op | source)
XLA Modules:
  0.0 190.4 jit_solution(9179475639104875036)
XLA Ops:
  0.6 0.8 select_reduce_fusion.2
  1.5 0.2 convert_reduce_fusion.1
  1.7 0.0 copy-start.2
  1.7 0.7 and_select_fusion.1
  2.5 0.7 and_select_fusion
  3.2 0.2 convert_reduce_fusion
  3.4 0.0 copy-start.3
  3.4 0.6 select_reduce_fusion
  4.0 3.5 %copy.15 = bf16[64,8,16,128]{3,1,2,0:T(8,128)(2,1)} copy(bf16[64,8,16,128]{3,2,1,0:T(8,128)(2,1)} %bitcast.14) | data formatting | bytes 4194304
  7.4 0.0 copy-done.2
  7.4 0.0 copy-done.3
  7.4 178.0 %train_step.1 = (bf16[16,512,128]{2,1,0:T(8,128)(2,1)}, bf16[512,256]{1,0:T(8,128)(2,1)}, f32[2048,128]{1,0:T(8,128)}, bf16[16,512,2048]{2,1,0:T(8,128)(2,1)}) custom-call(s32[24]{0:T(128)} %get-tuple-element.12.refs_0_, s32[16]{0:T(128)} %copy-done.3, s32[24]{0:T(128)} %get-tuple-element.11.refs_2_, s32[16]{0:T(128)} %copy-done.2, s32[8,8192]{1,0:T(8,128)} %bitcast.15, ...), custom_call_target="tpu_custom_call" | custom-call | tf_op jit(solution)/shard_map/train_step/pallas_call | solution.py:535
  185.5 0.0 copy-start.1
  185.5 0.0 copy-start
  185.5 3.2 %copy.19 = bf16[16,512,128]{2,1,0:T(8,128)(2,1)} copy(bf16[16,512,128]{2,1,0:T(8,128)(2,1)} %get-tuple-element.16) | data formatting | bytes 4194304
  188.7 0.0 copy-done.1
  188.7 0.7 copy.20
  189.4 0.0 copy-done
  189.4 1.0 copy.21
  (4 shorter events, 0.0 us)
Async XLA Ops:
  1.7 5.7 %copy-start.2 = (s32[16]{0:T(128)}, s32[16]{0:T(128)S(1)}, u32[]{:S(2)}) copy-start(s32[16]{0:T(128)S(1)} %multiply_add_fusion.1.refs_3_) | copy-start | bytes 196
  3.4 4.1 %copy-start.3 = (s32[16]{0:T(128)}, s32[16]{0:T(128)S(1)}, u32[]{:S(2)}) copy-start(s32[16]{0:T(128)S(1)} %multiply_add_fusion.refs_1_) | copy-start | bytes 196
  185.5 3.2 %copy-start.1 = (bf16[512,256]{1,0:T(8,128)(2,1)S(1)}, bf16[512,256]{1,0:T(8,128)(2,1)}, u32[]{:S(2)}) copy-start(bf16[512,256]{1,0:T(8,128)(2,1)} %get-tuple-element.17) | copy-start | bytes 786436
  185.5 3.9 %copy-start = (f32[2048,128]{1,0:T(8,128)S(1)}, f32[2048,128]{1,0:T(8,128)}, u32[]{:S(2)}) copy-start(f32[2048,128]{1,0:T(8,128)} %get-tuple-element.18) | copy-start | bytes 3145732

commit v4 on v3

--- a/solution.py
+++ b/solution.py
@@ -11,9 +11,10 @@
 BF = jnp.bfloat16
 F32 = jnp.float32
 MESH = pl.DeviceIdType.MESH
-PIECES = 4
+PIECES = 8
 HALVES = 2
 CHUNK = 16
+LAG = 3
 VMEM_LIMIT = 62 << 20
 BAG_GROUP = 32
 LOW = 256
@@ -38,7 +39,7 @@
 
     lax.fori_loop(1, n_node, by_node, 0)
     lax.fori_loop(1, n_local, by_lane, 0)
-    pl.semaphore_wait(barrier, n_node + n_local - 2)
+    return barrier
 
 
 def flatten_picks(idx_ref, size_ref, iota_ref, key_ref, low_ref):
@@ -96,7 +97,9 @@
     share = half // n_local
     width = r.gpre.shape[3]
     per_node = samples // BAG_GROUP
-    chunks = n_node * small // (CHUNK * BAG_GROUP)
+    groups = small // BAG_GROUP
+    at_once = CHUNK // groups
+    chunks = n_node // at_once
     arrived = [getattr(r, f"arrived{p}") for p in range(PIECES)]
     landed = [getattr(r, f"landed{p}") for p in range(PIECES)]
     returned = [getattr(r, f"returned{p}") for p in range(PIECES)]
@@ -168,30 +171,25 @@
         buffer = lax.rem(t, 2)
         return pltpu.make_async_copy(r.kept.at[t], r.counts.at[buffer], r.fetch_sem.at[buffer])
 
-    def pool_piece(p):
-        def one_chunk(c):
-            t = p * chunks + c
-
-            @pl.when(t >= 2)
-            def _():
-                save(t - 2).wait()
-
-            buffer = lax.rem(t, 2)
-            for i in range(CHUNK):
-                source = lax.rem(node + c * 4 + i // 4, n_node)
-                group = source * per_node + p * 4 + i % 4
-                put_counts(r.counts, buffer, i * BAG_GROUP, count_group(r.key, r.low, r.iota, group))
-            save(t).start()
-            sums = dot(r.counts[buffer], r.table[...]).astype(BF)
-            for i in range(4):
-                r.pooled[p, c * 4 + i] = sums[i * small : (i + 1) * small]
-            for piece in range(PIECES):
-
-                @pl.when(p == piece)
-                def _():
-                    each(c * 4 + 4, lambda k: out_node(piece, k).start(), jnp.maximum(c * 4, 1))
-
-        each(chunks, one_chunk)
+    def pool_chunk(p, c):
+        t = p * chunks + c
+
+        @pl.when(t >= 2)
+        def _():
+            save(t - 2).wait()
+
+        buffer = lax.rem(t, 2)
+        for i in range(CHUNK):
+            source = lax.rem(node + c * at_once + i // groups, n_node)
+            group = source * per_node + p * groups + i % groups
+            put_counts(r.counts, buffer, i * BAG_GROUP, count_group(r.key, r.low, r.iota, group))
+        save(t).start()
+        sums = dot(r.counts[buffer], r.table[...]).astype(BF)
+        for i in range(at_once):
+            r.pooled[p, c * at_once + i] = sums[i * small : (i + 1) * small]
+
+    def send_chunk(p, c):
+        each((c + 1) * at_once, lambda k: out_node(p, k).start(), jnp.maximum(c * at_once, 1))
 
     def pack_piece(p):
         each(n_node, lambda k: out_node(p, k).wait_recv(), 1)
@@ -371,8 +369,11 @@
         def one_chunk(c):
             t = p * chunks + c
             buffer = lax.rem(t, 2)
-            for i in range(4):
-                r.home_t[:, i * small : (i + 1) * small] = r.home[p, lax.rem(node + c * 4 + i, n_node)].T
+            for i in range(at_once * small // 128):
+                parts = [
+                    r.home[p, lax.rem(node + c * at_once + i * (128 // small) + j, n_node)] for j in range(128 // small)
+                ]
+                r.home_t[:, i * 128 : (i + 1) * 128] = jnp.concatenate(parts, 0).T
             fetch(t).wait()
             for n in range(r.sums.shape[1] // 512):
                 here = slice(n * 512, (n + 1) * 512)
@@ -391,63 +392,105 @@
         pltpu.make_async_copy(r.weight_hbm, r.weight, r.load_sem.at[2]),
         pltpu.make_async_copy(r.grad_hbm.at[:, my_columns], r.hgrad, r.load_sem.at[3]),
     ]
+    barrier = greet(n_node, n_local, node, lane)
+    fill = [
+        pltpu.make_async_copy(r.idx_hbm, r.idx, r.load_sem.at[4]),
+        pltpu.make_async_copy(r.size_hbm, r.size, r.load_sem.at[5]),
+        pltpu.make_async_copy(r.table_hbm, r.table, r.load_sem.at[6]),
+    ]
+    for load in fill:
+        load.start()
+    for load in fill:
+        load.wait()
     for load in loads:
         load.start()
-    greet(n_node, n_local, node, lane)
     flatten_picks(r.idx, r.size, r.iota, r.key, r.low)
-    r.sums[...] = jnp.zeros_like(r.sums)
+    each(chunks, lambda c: pool_chunk(0, c))
+    pl.semaphore_wait(barrier, n_node + n_local - 2)
+    for c in range(chunks):
+        send_chunk(0, c)
 
     def turn(p):
-        pool_piece(p)
-        for piece in range(PIECES - 1):
-
-            @pl.when(p == piece + 1)
+        def one_chunk(c):
+            pool_chunk(p, c)
+            for piece in range(1, PIECES):
+
+                @pl.when(p == piece)
+                def _():
+                    send_chunk(piece, c)
+
+        each(chunks, one_chunk)
+        for piece in range(PIECES - LAG):
+
+            @pl.when(p == piece + LAG)
             def _():
                 pack_piece(piece)
 
-    each(PIECES, turn)
-    pack_piece(PIECES - 1)
+    each(PIECES, turn, 1)
+    r.sums[...] = jnp.zeros_like(r.sums)
     for t in range(2):
         save(PIECES * chunks - 2 + t).wait()
     for t in range(2):
         fetch(t).start()
     for load in loads:
         load.wait()
-    per_half = PIECES // HALVES
-    for h in range(HALVES):
-        for p in range(h * per_half, (h + 1) * per_half):
-            unpack_piece(p)
-        low_parts(h)
-    for h in range(HALVES):
-        reduce_parts(0, h)
-    for h in range(HALVES):
-        cross(h)
-        pre(h)
-    for h in range(HALVES):
-        activate(h)
+    unpack_piece(2)
+    unpack_piece(1)
+    unpack_piece(0)
+    unpack_piece(3)
+    low_parts(0)
+    pack_piece(5)
+    reduce_parts(0, 0)
+    pack_piece(7)
+    cross(0)
+    pre(0)
+    unpack_piece(5)
+    pack_piece(6)
+    unpack_piece(4)
+    activate(0)
+    unpack_piece(6)
+    unpack_piece(7)
+    low_parts(1)
     back_chips(0, [0])
     pass_on(0)
+    reduce_parts(0, 1)
     back_chips(0, [1, 2, 3])
-    pass_on(1)
     rank_grad(0)
-    back_chips(1, [0, 1, 2, 3])
+    cross(1)
+    pre(1)
     reduce_parts(1, 0)
-    rank_grad(1)
+    activate(1)
+    back_chips(1, [0])
     input_grad(0)
     pack_back(0)
     pack_back(1)
+    pass_on(1)
+    back_chips(1, [1, 2, 3])
+    rank_grad(1)
+    pack_back(2)
+    route_piece(0)
     reduce_parts(1, 1)
+    pack_back(3)
+    route_piece(2)
+    route_piece(1)
     input_grad(1)
-    pack_back(2)
-    pack_back(3)
-    route_piece(0)
-    route_piece(1)
+    pack_back(4)
+    route_piece(3)
+    pack_back(5)
+    pack_back(6)
     add_piece(0)
-    route_piece(2)
+    route_piece(4)
     add_piece(1)
-    route_piece(3)
+    pack_back(7)
+    route_piece(5)
+    route_piece(6)
     add_piece(2)
+    route_piece(7)
     add_piece(3)
+    add_piece(4)
+    add_piece(5)
+    add_piece(6)
+    add_piece(7)
     for n in range(r.sums.shape[1] // 128):
         r.table_grad[n * 128 : (n + 1) * 128, :] = r.sums[:, n * 128 : (n + 1) * 128].T
 
@@ -473,8 +516,8 @@
 def train_step(operands, features, samples, n_node, n_local, cap):
     depth, hidden = operands["down_hbm"].shape[1], operands["weight_hbm"].shape[1]
     total = operands["down_hbm"].shape[0]
-    table_rows, emb = operands["table"].shape
-    groups = operands["idx"].shape[1] // BAG_GROUP
+    table_rows, emb = operands["table_hbm"].shape
+    groups = operands["idx_hbm"].shape[1] // BAG_GROUP
     small, half, width, chips = samples // PIECES, samples // HALVES, hidden // n_local, n_local // 2
     kept = (groups // CHUNK, CHUNK * BAG_GROUP, table_rows)
     outs = {
@@ -486,6 +529,9 @@
     parts = pltpu.VMEM((2, HALVES, n_local, half // n_local, depth), BF)
     quarter = pltpu.VMEM((HALVES, chips, half, width), BF)
     scratch = {
+        "idx": pltpu.VMEM(operands["idx_hbm"].shape, jnp.int32),
+        "size": pltpu.VMEM(operands["size_hbm"].shape, jnp.int32),
+        "table": pltpu.VMEM((table_rows, emb), BF),
         "iota": pltpu.VMEM((LOW, LOW), BF),
         "key": pltpu.VMEM((groups, LOW), F32),
         "low": pltpu.VMEM((groups, LOW), F32),
@@ -493,7 +539,7 @@
         "pooled": pltpu.VMEM((PIECES, n_node, small, emb), BF),
         "packed": pltpu.VMEM((PIECES, n_local, cap, small, emb), BF),
         "home": pltpu.VMEM((PIECES, n_node, small, emb), BF),
-        "home_t": pltpu.VMEM((emb, 4 * small), BF),
+        "home_t": pltpu.VMEM((emb, kept[1]), BF),
         "sums": pltpu.VMEM((emb, table_rows), F32),
         "x": pltpu.VMEM((samples, total), BF),
         "down": pltpu.VMEM((total, depth), BF),
@@ -512,7 +558,7 @@
         "pre_recv": quarter,
         "pre_own": pltpu.VMEM((HALVES, half, width), F32),
         "gpre": pltpu.VMEM((HALVES, n_local, half, width), BF),
-        "load_sem": SEM((4,)),
+        "load_sem": SEM((7,)),
         "save_sem": SEM((2,)),
         "fetch_sem": SEM((2,)),
     }
@@ -594,9 +640,9 @@
         "slot": owner_slot,
         "back_pick": back_source,
         "back_slot": source_slot,
-        "idx": indices[0].T,
-        "size": bag_sizes,
-        "table": tables,
+        "idx_hbm": indices[0].T,
+        "size_hbm": bag_sizes,
+        "table_hbm": tables,
         "bias": cross_bias.reshape(1, -1),
         "hbias": mlp_bias.reshape(1, -1),
         "grad_hbm": hidden_grad,

time: 191 us -> 179 us (0.937)
  Pallas kernels: 178 us -> 167 us
    pallas_call x1, Pallas kernels: 178 us -> 167 us  [train_step(): pl.pallas_call(functools.partial(step_kernel, names, n_node, n_local), ou...]
where the time goes in v4:
time: 179 us
  Pallas kernels  167 us (93%)
  local copies, waits for them, and re-layouts  8.35 us (5%)
  other arithmetic  3.32 us (2%)
    pallas_call x1, Pallas kernels, train_step(): pl.pallas_call(functools.partial(step_kernel, names, n_node, n_local), ou...  167 us
    unnamed x12, local copies, waits for them, and re-layouts  8.35 us

profile of v4, /device:TPU:1, one launch (start us, length us, event | category | flops | bytes accessed | tf_op | source)
XLA Modules:
  0.0 179.2 jit_solution(12917857660698125828)
XLA Ops:
  0.6 0.8 select_reduce_fusion.2
  1.5 0.2 convert_reduce_fusion.1
  1.7 0.0 copy-start.2
  1.7 0.7 and_select_fusion.1
  2.5 0.7 and_select_fusion
  3.2 0.2 convert_reduce_fusion
  3.4 0.0 copy-start.3
  3.4 0.6 select_reduce_fusion
  4.0 3.5 %copy.15 = bf16[64,8,16,128]{3,1,2,0:T(8,128)(2,1)} copy(bf16[64,8,16,128]{3,2,1,0:T(8,128)(2,1)} %bitcast.14) | data formatting | bytes 4194304
  7.4 0.0 copy-done.2
  7.4 0.0 copy-done.3
  7.4 166.8 %train_step.1 = (bf16[16,512,128]{2,1,0:T(8,128)(2,1)}, bf16[512,256]{1,0:T(8,128)(2,1)}, f32[2048,128]{1,0:T(8,128)}, bf16[16,512,2048]{2,1,0:T(8,128)(2,1)}) custom-call(s32[24]{0:T(128)} %get-tuple-element.12.refs_0_, s32[16]{0:T(128)} %copy-done.3, s32[24]{0:T(128)} %get-tuple-element.11.refs_2_, s32[16]{0:T(128)} %copy-done.2, s32[8,8192]{1,0:T(8,128)} %bitcast.15, ...), custom_call_target="tpu_custom_call" | custom-call | tf_op jit(solution)/shard_map/train_step/pallas_call | solution.py:581
  174.2 0.0 copy-start.1
  174.3 0.0 copy-start
  174.3 3.2 %copy.19 = bf16[16,512,128]{2,1,0:T(8,128)(2,1)} copy(bf16[16,512,128]{2,1,0:T(8,128)(2,1)} %get-tuple-element.16) | data formatting | bytes 4194304
  177.5 0.0 copy-done.1
  177.5 0.7 copy.20
  178.2 0.0 copy-done
  178.2 1.0 copy.21
  (4 shorter events, 0.0 us)
Async XLA Ops:
  1.7 5.7 %copy-start.2 = (s32[16]{0:T(128)}, s32[16]{0:T(128)S(1)}, u32[]{:S(2)}) copy-start(s32[16]{0:T(128)S(1)} %multiply_add_fusion.1.refs_3_) | copy-start | bytes 196
  3.4 4.1 %copy-start.3 = (s32[16]{0:T(128)}, s32[16]{0:T(128)S(1)}, u32[]{:S(2)}) copy-start(s32[16]{0:T(128)S(1)} %multiply_add_fusion.refs_1_) | copy-start | bytes 196
  174.2 3.2 %copy-start.1 = (bf16[512,256]{1,0:T(8,128)(2,1)S(1)}, bf16[512,256]{1,0:T(8,128)(2,1)}, u32[]{:S(2)}) copy-start(bf16[512,256]{1,0:T(8,128)(2,1)} %get-tuple-element.17) | copy-start | bytes 786436
  174.3 3.9 %copy-start = (f32[2048,128]{1,0:T(8,128)S(1)}, f32[2048,128]{1,0:T(8,128)}, u32[]{:S(2)}) copy-start(f32[2048,128]{1,0:T(8,128)} %get-tuple-element.18) | copy-start | bytes 3145732

commit v5 on v4

--- a/solution.py
+++ b/solution.py
@@ -14,7 +14,7 @@
 PIECES = 8
 HALVES = 2
 CHUNK = 16
-LAG = 3
+LAG = 2
 VMEM_LIMIT = 62 << 20
 BAG_GROUP = 32
 LOW = 256
@@ -129,6 +129,31 @@
     def chip_peer(dy):
         return node, lax.rem(chip + dy, chips) * 2 + core
 
+    def find_slots():
+        features = r.owner.shape[1]
+        wide = (features, features)
+        here = jnp.broadcast_to(r.owner[...].astype(F32), wide)
+        owner, other = here.T.astype(jnp.int32), here.astype(jnp.int32)
+        feature, at = lax.broadcasted_iota(jnp.int32, wide, 0), lax.broadcasted_iota(jnp.int32, wide, 1)
+        group, other_group = feature // n_node, at // n_node
+        own_lane, own_node = lax.rem(owner, n_local), owner // n_local
+        ahead = (at < feature) & (group == other_group) & (lax.rem(other, n_local) == own_lane)
+        rank = jnp.sum(ahead.astype(F32), axis=1, keepdims=True).astype(jnp.int32)
+        source_slot, target_slot = group * cap + rank, own_lane * cap + rank
+
+        def put(row, where, value, limit):
+            chosen = jnp.where(where, value, 0).astype(F32)
+            found = jnp.sum(chosen, axis=0, keepdims=True).astype(jnp.int32)
+            r.slots_v[row : row + 1, :] = jnp.clip(found, 0, limit - 1)
+
+        put(0, (own_lane == lane) & (source_slot == at), own_node, n_node)
+        put(1, feature == lane * n_node + at, target_slot, n_local * cap)
+        put(2, (group == lane) & (target_slot == at), feature - lane * n_node, n_node)
+        put(3, owner == at * n_local + lane, source_slot, n_local * cap)
+        copy = pltpu.make_async_copy(r.slots_v, r.slots, r.load_sem.at[7])
+        copy.start()
+        copy.wait()
+
     def out_node(p, k):
         return remote(r.pooled.at[p, k], arrived[p].at[node], (r.on_s, r.on_r), (p, k), node_peer(k))
 
@@ -198,17 +223,27 @@
         def send(d):
             target = lax.rem(lane + d, n_local)
             for c in range(cap):
-                r.packed[p, d, c] = arrived[p][r.pick[target * cap + c]]
+                r.packed[p, d, c] = arrived[p][r.slots[0, target * cap + c]]
             out_lane(p, d).start()
 
         each(n_local, send, 1)
         for c in range(cap):
-            landed[p][lane * cap + c] = arrived[p][r.pick[lane * cap + c]]
+            landed[p][lane * cap + c] = arrived[p][r.slots[0, lane * cap + c]]
 
     def unpack_piece(p):
         each(n_local, lambda d: out_lane(p, d).wait_recv(), 1)
         for q in range(n_node):
-            r.x[p * small : (p + 1) * small, q * 128 : (q + 1) * 128] = landed[p][r.slot[q]]
+            r.x[p * small : (p + 1) * small, q * 128 : (q + 1) * 128] = landed[p][r.slots[1, q]]
+
+    def lay_up():
+        depth = r.up.shape[0] // r.gx.shape[0]
+
+        def block(i):
+            turned = jnp.swapaxes(r.gx[i].reshape(depth, n_node, 128), 0, 1)
+            for q in range(n_node):
+                r.up[pl.ds(pl.multiple_of(i * depth, depth), depth), q * 128 : (q + 1) * 128] = turned[q]
+
+        each(r.gx.shape[0], block)
 
     def send_parts(w, h, part):
         def columns(n):
@@ -251,6 +286,10 @@
                 r.crossed[n * 4 + i, rows(h), :] = result[:, i * 128 : (i + 1) * 128]
 
         each(total // 512, columns)
+        keep_crossed(h).start()
+
+    def keep_crossed(h):
+        return pltpu.make_async_copy(r.crossed.at[:, rows(h)], r.crossed_out.at[:, rows(h)], r.out_sem.at[h])
 
     def pre(h):
         def part(t):
@@ -345,23 +384,23 @@
         def send(d):
             target = lax.rem(lane + d, n_local)
             for c in range(cap):
-                r.packed[p, d, c] = r.gx[r.back_pick[target * cap + c], here]
+                r.packed[p, d, c] = r.gx[r.slots[2, target * cap + c], here]
             back_lane(p, d).start()
 
         each(n_local, send, 1)
         for c in range(cap):
-            returned[p][lane * cap + c] = r.gx[r.back_pick[lane * cap + c], here]
+            returned[p][lane * cap + c] = r.gx[r.slots[2, lane * cap + c], here]
 
     def route_piece(p):
         each(n_node, lambda k: out_node(p, k).wait_send(), 1)
         each(n_local, lambda d: back_lane(p, d).wait_recv(), 1)
 
         def send(k):
-            r.pooled[p, k] = returned[p][r.back_slot[lax.rem(node + k, n_node)]]
+            r.pooled[p, k] = returned[p][r.slots[3, lax.rem(node + k, n_node)]]
             back_node(p, k).start()
 
         each(n_node, send, 1)
-        r.home[p, node] = returned[p][r.back_slot[node]]
+        r.home[p, node] = returned[p][r.slots[3, node]]
 
     def add_piece(p):
         each(n_node, lambda k: back_node(p, k).wait_recv(), 1)
@@ -388,7 +427,7 @@
     my_columns = pl.ds(pl.multiple_of(lane * width, width), width)
     loads = [
         pltpu.make_async_copy(r.down_hbm, r.down, r.load_sem.at[0]),
-        pltpu.make_async_copy(r.up_hbm, r.up, r.load_sem.at[1]),
+        pltpu.make_async_copy(r.up_hbm, r.gx, r.load_sem.at[1]),
         pltpu.make_async_copy(r.weight_hbm, r.weight, r.load_sem.at[2]),
         pltpu.make_async_copy(r.grad_hbm.at[:, my_columns], r.hgrad, r.load_sem.at[3]),
     ]
@@ -400,6 +439,8 @@
     ]
     for load in fill:
         load.start()
+    r.slots_v[...] = jnp.zeros_like(r.slots_v)
+    find_slots()
     for load in fill:
         load.wait()
     for load in loads:
@@ -434,23 +475,23 @@
         fetch(t).start()
     for load in loads:
         load.wait()
+    unpack_piece(0)
+    unpack_piece(1)
+    unpack_piece(3)
     unpack_piece(2)
-    unpack_piece(1)
-    unpack_piece(0)
-    unpack_piece(3)
     low_parts(0)
-    pack_piece(5)
+    pack_piece(6)
+    unpack_piece(5)
+    unpack_piece(4)
+    lay_up()
     reduce_parts(0, 0)
     pack_piece(7)
+    unpack_piece(6)
     cross(0)
     pre(0)
-    unpack_piece(5)
-    pack_piece(6)
-    unpack_piece(4)
-    activate(0)
-    unpack_piece(6)
     unpack_piece(7)
     low_parts(1)
+    activate(0)
     back_chips(0, [0])
     pass_on(0)
     reduce_parts(0, 1)
@@ -467,8 +508,8 @@
     pass_on(1)
     back_chips(1, [1, 2, 3])
     rank_grad(1)
+    route_piece(0)
     pack_back(2)
-    route_piece(0)
     reduce_parts(1, 1)
     pack_back(3)
     route_piece(2)
@@ -477,9 +518,9 @@
     pack_back(4)
     route_piece(3)
     pack_back(5)
+    route_piece(4)
     pack_back(6)
     add_piece(0)
-    route_piece(4)
     add_piece(1)
     pack_back(7)
     route_piece(5)
@@ -498,6 +539,7 @@
         each(n_node, lambda k: back_node(p, k).wait_send(), 1)
         each(n_local, lambda d: back_lane(p, d).wait_send(), 1)
     for h in range(HALVES):
+        keep_crossed(h).wait()
         for w in range(2):
             each(n_local, lambda d: part_to(w, h, d).wait_send(), 1)
             each(n_local, lambda d: share_to(w, h, d).wait_send(), 1)
@@ -507,7 +549,6 @@
         each(chips, lambda dy: forward(h, dy).wait_send())
 
 
-SMEM = pl.BlockSpec(memory_space=pltpu.SMEM)
 VMEM = pl.BlockSpec(memory_space=pltpu.VMEM)
 ANY = pl.BlockSpec(memory_space=pl.ANY)
 SEM = pltpu.SemaphoreType.DMA
@@ -521,7 +562,7 @@
     small, half, width, chips = samples // PIECES, samples // HALVES, hidden // n_local, n_local // 2
     kept = (groups // CHUNK, CHUNK * BAG_GROUP, table_rows)
     outs = {
-        "crossed": (jax.ShapeDtypeStruct((features, samples, emb), BF), VMEM),
+        "crossed_out": (jax.ShapeDtypeStruct((features, samples, emb), BF), ANY),
         "hidden": (jax.ShapeDtypeStruct((samples, width), BF), VMEM),
         "table_grad": (jax.ShapeDtypeStruct((table_rows, emb), F32), VMEM),
         "kept": (jax.ShapeDtypeStruct(kept, BF), ANY),
@@ -532,6 +573,8 @@
         "idx": pltpu.VMEM(operands["idx_hbm"].shape, jnp.int32),
         "size": pltpu.VMEM(operands["size_hbm"].shape, jnp.int32),
         "table": pltpu.VMEM((table_rows, emb), BF),
+        "slots_v": pltpu.VMEM((8, operands["owner"].shape[1]), jnp.int32),
+        "slots": pltpu.SMEM((8, operands["owner"].shape[1]), jnp.int32),
         "iota": pltpu.VMEM((LOW, LOW), BF),
         "key": pltpu.VMEM((groups, LOW), F32),
         "low": pltpu.VMEM((groups, LOW), F32),
@@ -549,6 +592,8 @@
         "term": pltpu.VMEM((samples, total), F32),
         "gcross": pltpu.VMEM((samples, total), F32),
         "gx": pltpu.VMEM((features, samples, emb), BF),
+        "crossed": pltpu.VMEM((features, samples, emb), BF),
+        "out_sem": SEM((HALVES,)),
         "rank_send": parts,
         "rank_recv": parts,
         "rank": parts,
@@ -558,7 +603,7 @@
         "pre_recv": quarter,
         "pre_own": pltpu.VMEM((HALVES, half, width), F32),
         "gpre": pltpu.VMEM((HALVES, n_local, half, width), BF),
-        "load_sem": SEM((7,)),
+        "load_sem": SEM((8,)),
         "save_sem": SEM((2,)),
         "fetch_sem": SEM((2,)),
     }
@@ -575,8 +620,7 @@
         for name in names:
             scratch[name + "_s"] = SEM(shape)
             scratch[name + "_r"] = SEM(shape)
-    places = {"pick": SMEM, "slot": SMEM, "back_pick": SMEM, "back_slot": SMEM}
-    specs = [places.get(name, ANY if name.endswith("_hbm") else VMEM) for name in operands]
+    specs = [ANY if name.endswith("_hbm") else VMEM for name in operands]
     names = [*operands, *outs, *scratch]
     return pl.pallas_call(
         functools.partial(step_kernel, names, n_node, n_local),
@@ -587,6 +631,38 @@
         compiler_params=pltpu.CompilerParams(collective_id=0, has_side_effects=True, vmem_limit_bytes=VMEM_LIMIT),
         name="train_step",
     )(*operands.values())
+
+
+def hand_out_kernel(count, *refs):
+    given, taken, held = refs[:count], refs[count : 2 * count], refs[2 * count : 3 * count]
+    read_sem, write_sem = refs[3 * count :]
+    reads, writes = [], []
+    for source, target, middle in zip(given, taken, held):
+        rows = source.shape[0] // 4
+        for i in range(4):
+            part, at = pl.ds(i * rows, rows), len(reads)
+            reads.append(pltpu.make_async_copy(source.at[part], middle.at[part], read_sem.at[at]))
+            writes.append(pltpu.make_async_copy(middle.at[part], target.at[part], write_sem.at[at]))
+    for copy in reads:
+        copy.start()
+    for read, write in zip(reads, writes):
+        read.wait()
+        write.start()
+    for copy in writes:
+        copy.wait()
+
+
+def hand_out(*arrays):
+    count = len(arrays)
+    return pl.pallas_call(
+        functools.partial(hand_out_kernel, count),
+        out_shape=[jax.ShapeDtypeStruct(a.shape, a.dtype) for a in arrays],
+        in_specs=[ANY] * count,
+        out_specs=[ANY] * count,
+        scratch_shapes=[*[pltpu.VMEM(a.shape, a.dtype) for a in arrays], SEM((4 * count,)), SEM((4 * count,))],
+        compiler_params=pltpu.CompilerParams(vmem_limit_bytes=16 << 20),
+        name="hand_out",
+    )(*arrays)
 
 
 def on_device(
@@ -603,55 +679,23 @@
 ):
     node_count = lax.axis_size("node")
     lane_count = lax.axis_size("local")
-    my_lane = lax.axis_index("local")
     capacity = node_count // lane_count + 1
-    slot_total = lane_count * capacity
     samples = hidden_grad.shape[0]
     hidden_width = hidden_grad.shape[1]
-    feat_ids = jnp.arange(owner_map.shape[0], dtype=jnp.int32)
-    node_ids = jnp.arange(node_count, dtype=jnp.int32)
-    source_dev = node_ids * lane_count + my_lane
-    source_feat = jnp.sum(
-        jnp.where(owner_map[None, :] == source_dev[:, None], feat_ids[None, :], 0), axis=1
-    )
-    source_group = source_feat // node_count
-    same_group = source_group[:, None] == source_group[None, :]
-    earlier = node_ids[None, :] < node_ids[:, None]
-    source_slot = source_group * capacity + jnp.sum(
-        (same_group & earlier).astype(jnp.int32), axis=1
-    )
-    group_owners = lax.dynamic_slice_in_dim(owner_map, my_lane * node_count, node_count)
-    owner_lane = group_owners % lane_count
-    owner_node = group_owners // lane_count
-    ahead_same = (owner_lane[:, None] == owner_lane[None, :]) & (
-        owner_node[None, :] < owner_node[:, None]
-    )
-    owner_slot = owner_lane * capacity + jnp.sum(ahead_same.astype(jnp.int32), axis=1)
-    slot_ids = jnp.arange(slot_total, dtype=jnp.int32)
-    pick_source = jnp.sum(
-        jnp.where(source_slot[None, :] == slot_ids[:, None], node_ids[None, :], 0), axis=1
-    )
-    back_source = jnp.sum(
-        jnp.where(owner_slot[None, :] == slot_ids[:, None], node_ids[None, :], 0), axis=1
-    )
-
     operands = {
-        "pick": pick_source,
-        "slot": owner_slot,
-        "back_pick": back_source,
-        "back_slot": source_slot,
+        "owner": owner_map.reshape(1, -1),
+        "bias": cross_bias.reshape(1, -1),
+        "hbias": mlp_bias.reshape(1, -1),
         "idx_hbm": indices[0].T,
         "size_hbm": bag_sizes,
         "table_hbm": tables,
-        "bias": cross_bias.reshape(1, -1),
-        "hbias": mlp_bias.reshape(1, -1),
         "grad_hbm": hidden_grad,
         "down_hbm": cross_down.reshape(-1, cross_down.shape[2]),
-        "up_hbm": cross_up.reshape(cross_up.shape[0], -1),
+        "up_hbm": cross_up.reshape(node_count, -1, cross_up.shape[2]),
         "weight_hbm": mlp_weight.reshape(-1, hidden_width),
     }
     crossed, hidden, table_grad, _ = train_step(operands, node_count, samples, node_count, lane_count, capacity)
-    return (crossed, hidden, table_grad)
+    return hand_out(crossed, hidden, table_grad)
 
 
 def solution(mesh):

time: 179 us -> 174 us (0.972)
  local copies, waits for them, and re-layouts: 8.35 us -> 3.76 us
  other arithmetic: 3.32 us -> 0 us
  Pallas kernels: 167 us -> 169 us
    unnamed x12 -> x6, local copies, waits for them, and re-layouts: 8.35 us -> 3.76 us
    pallas_call x0 -> x1, Pallas kernels: none -> 2.5 us  [hand_out(): pl.pallas_call(functools.partial(hand_out_kernel, count), out_shape=[jax....]
    reduce_sum x4 -> x0, other arithmetic: 1.81 us -> none  [the longest x1 0.84 us: on_device(): jnp.sum(jnp.where(owner_map[None, :] == source_dev[:, None], feat_ids[Non...]
where the time goes in v5:
time: 174 us; the launch traced here: 173 us
  Pallas kernels  169 us (97%)
  local copies, waits for them, and re-layouts  3.76 us (2%)
    pallas_call x1, Pallas kernels, train_step(): pl.pallas_call(functools.partial(step_kernel, names, n_node, n_local), ou...  166 us
    unnamed x6, local copies, waits for them, and re-layouts  3.76 us

profile of v5, /device:TPU:1, one launch (start us, length us, event | category | flops | bytes accessed | tf_op | source)
XLA Modules:
  0.0 173.5 jit_solution(101049202873861626)
XLA Ops:
  0.6 166.4 %train_step.1 = (bf16[16,512,128]{2,1,0:T(8,128)(2,1)}, bf16[512,256]{1,0:T(8,128)(2,1)}, f32[2048,128]{1,0:T(8,128)}, bf16[16,512,2048]{2,1,0:T(8,128)(2,1)}) custom-call(s32[1,128]{1,0:T(1,128)} %bitcast.15, f32[1,2048]{1,0:T(1,128)} %bitcast.13, f32[1,2048]{1,0:T(1,128)} %bitcast.14, s32[8,8192]{1,0:T(8,128)} %bitcast.12, s32[1,8192]{1,0:T(1,128)} %refs_4_.1, ...), custom_call_target="tpu_custom_call" | custom-call | tf_op jit(solution)/shard_map/train_step/pallas_call | solution.py:625
  167.1 0.0 copy-start
  167.1 1.6 copy-done
  168.6 0.0 copy-start.1
  168.7 1.2 copy-done.1
  169.9 0.0 copy-start.2
  169.9 0.9 copy-done.2
  170.8 2.5 %hand_out.1 = (bf16[16,512,128]{2,1,0:T(8,128)(2,1)}, bf16[512,256]{1,0:T(8,128)(2,1)}, f32[2048,128]{1,0:T(8,128)}) custom-call(bf16[16,512,128]{2,1,0:T(8,128)(2,1)S(1)} %copy-done, bf16[512,256]{1,0:T(8,128)(2,1)S(1)} %copy-done.2, f32[2048,128]{1,0:T(8,128)S(1)} %copy-done.1), custom_call_target="tpu_custom_call" | custom-call | tf_op jit(solution)/shard_map/hand_out/pallas_call | solution.py:657
Async XLA Ops:
  167.1 1.6 copy-start
  168.6 1.2 copy-start.1
  169.9 0.9 copy-start.2

commit v6 on v5

--- a/solution.py
+++ b/solution.py
@@ -660,7 +660,7 @@
         in_specs=[ANY] * count,
         out_specs=[ANY] * count,
         scratch_shapes=[*[pltpu.VMEM(a.shape, a.dtype) for a in arrays], SEM((4 * count,)), SEM((4 * count,))],
-        compiler_params=pltpu.CompilerParams(vmem_limit_bytes=16 << 20),
+        compiler_params=pltpu.CompilerParams(vmem_limit_bytes=VMEM_LIMIT),
         name="hand_out",
     )(*arrays)
 

time: 174 us -> 171 us (0.983)
  local copies, waits for them, and re-layouts: 3.76 us -> 0 us
    unnamed x6 -> x0, local copies, waits for them, and re-layouts: 3.76 us -> none
where the time goes in v6:
time: 171 us; the launch traced here: 170 us
  Pallas kernels  169 us (99%)
    pallas_call x1, Pallas kernels, train_step(): pl.pallas_call(functools.partial(step_kernel, names, n_node, n_local), ou...  166 us

profile of v6, /device:TPU:1, one launch (start us, length us, event | category | flops | bytes accessed | tf_op | source)
XLA Modules:
  0.0 170.2 jit_solution(17649895114822586059)
XLA Ops:
  0.6 166.4 %train_step.1 = (bf16[16,512,128]{2,1,0:T(8,128)(2,1)}, bf16[512,256]{1,0:T(8,128)(2,1)}, f32[2048,128]{1,0:T(8,128)}, bf16[16,512,2048]{2,1,0:T(8,128)(2,1)}) custom-call(s32[1,128]{1,0:T(1,128)} %bitcast.15, f32[1,2048]{1,0:T(1,128)} %bitcast.13, f32[1,2048]{1,0:T(1,128)} %bitcast.14, s32[8,8192]{1,0:T(8,128)} %bitcast.12, s32[1,8192]{1,0:T(1,128)} %refs_4_.1, ...), custom_call_target="tpu_custom_call" | custom-call | tf_op jit(solution)/shard_map/train_step/pallas_call | solution.py:625
  167.1 3.0 %hand_out.1 = (bf16[16,512,128]{2,1,0:T(8,128)(2,1)}, bf16[512,256]{1,0:T(8,128)(2,1)}, f32[2048,128]{1,0:T(8,128)}) custom-call(bf16[16,512,128]{2,1,0:T(8,128)(2,1)} %get-tuple-element.6.refs_0_, bf16[512,256]{1,0:T(8,128)(2,1)} %get-tuple-element.7.refs_1_, f32[2048,128]{1,0:T(8,128)} %get-tuple-element.8.refs_2_), custom_call_target="tpu_custom_call" | custom-call | tf_op jit(solution)/shard_map/hand_out/pallas_call | solution.py:657

commit v7 on v6

--- a/solution.py
+++ b/solution.py
@@ -512,23 +512,23 @@
     pack_back(2)
     reduce_parts(1, 1)
     pack_back(3)
-    route_piece(2)
     route_piece(1)
     input_grad(1)
     pack_back(4)
+    pack_back(5)
+    route_piece(2)
+    add_piece(0)
     route_piece(3)
-    pack_back(5)
-    route_piece(4)
     pack_back(6)
-    add_piece(0)
     add_piece(1)
     pack_back(7)
+    route_piece(4)
+    add_piece(2)
+    add_piece(3)
     route_piece(5)
+    add_piece(4)
     route_piece(6)
-    add_piece(2)
     route_piece(7)
-    add_piece(3)
-    add_piece(4)
     add_piece(5)
     add_piece(6)
     add_piece(7)

time: 171 us -> 168 us (0.982)
  Pallas kernels: 169 us -> 167 us
    pallas_call x1, Pallas kernels: 166 us -> 164 us  [train_step(): pl.pallas_call(functools.partial(step_kernel, names, n_node, n_local), ou...]
where the time goes in v7:
time: 168 us
  Pallas kernels  167 us (99%)
    pallas_call x1, Pallas kernels, train_step(): pl.pallas_call(functools.partial(step_kernel, names, n_node, n_local), ou...  164 us

profile of v7, /device:TPU:1, one launch (start us, length us, event | category | flops | bytes accessed | tf_op | source)
XLA Modules:
  0.0 168.1 jit_solution(7103487980002725595)
XLA Ops:
  0.6 164.3 %train_step.1 = (bf16[16,512,128]{2,1,0:T(8,128)(2,1)}, bf16[512,256]{1,0:T(8,128)(2,1)}, f32[2048,128]{1,0:T(8,128)}, bf16[16,512,2048]{2,1,0:T(8,128)(2,1)}) custom-call(s32[1,128]{1,0:T(1,128)} %bitcast.15, f32[1,2048]{1,0:T(1,128)} %bitcast.13, f32[1,2048]{1,0:T(1,128)} %bitcast.14, s32[8,8192]{1,0:T(8,128)} %bitcast.12, s32[1,8192]{1,0:T(1,128)} %refs_4_.1, ...), custom_call_target="tpu_custom_call" | custom-call | tf_op jit(solution)/shard_map/train_step/pallas_call | solution.py:625
  164.9 3.0 %hand_out.1 = (bf16[16,512,128]{2,1,0:T(8,128)(2,1)}, bf16[512,256]{1,0:T(8,128)(2,1)}, f32[2048,128]{1,0:T(8,128)}) custom-call(bf16[16,512,128]{2,1,0:T(8,128)(2,1)} %get-tuple-element.6.refs_0_, bf16[512,256]{1,0:T(8,128)(2,1)} %get-tuple-element.7.refs_1_, f32[2048,128]{1,0:T(8,128)} %get-tuple-element.8.refs_2_), custom_call_target="tpu_custom_call" | custom-call | tf_op jit(solution)/shard_map/hand_out/pallas_call | solution.py:657
